TPU v7x, 512 devices: a whole 4x4x16 slice. The times are simulated.
512 devices in a mesh: snap: 8 (over x, core), node: 64 (over y, z).
Axes of the slice: x: 4, y: 4, z: 16, core: 2. Of those that a mesh axis runs over, the one named last changes fastest.
Arguments:
- features: bfloat16 [8, 65536, 512], P('snap', 'node'), may hold values from -6 to 6
- tile_rows: int32 [8, 1792], P('snap', 'node'), may hold values from 0 to 511, as said below
- tile_cols: int32 [8, 1792], P('snap', 'node'), may hold values from 0 to 511, as said below
- tile_values: bfloat16 [8, 1792, 128, 128], P('snap', 'node'), may hold values from -0.125 to 0.125
- tile_count: int32 [8, 64], P('snap', 'node'), may hold values from 9 to 28, as said below
- w_graph: bfloat16 [512, 512], replicated, may hold values from -0.25 to 0.25
- norm_gain: float32 [512], replicated, may hold values from 0.5 to 1.5
- w_query: bfloat16 [512, 512], replicated
- w_key: bfloat16 [512, 512], replicated, may hold values from -0.25 to 0.25
- w_value: bfloat16 [512, 512], replicated, may hold values from -0.25 to 0.25
- w_out: bfloat16 [512, 512], replicated, may hold values from -0.25 to 0.25
Outputs:
- layer_out: bfloat16 [8, 65536, 512], P(None, ('node', 'snap'))
Inputs may be any that keep to these rules, and one draw needn't show every extreme that they name: `tile_rows`: every slot held by node index j (slots j * 28 to (j + 1) * 28 - 1) names a row block of that index's own nodes. `tile_cols`: every slot held by node index j names a column block of the nodes held by node indices j - 2 to j + 2. Of each node index's slots, the first tile_count are live and the rest are ignored; in each snapshot some node index has all 28 live.
All inputs are finite; a program needn't handle non-finite values.
Results may differ from a plain program's by a relative error of at most 0.0086.
Values may be sent and summed in bfloat16 or wider, within the bound.
A program may use at most 64 MiB of HBM per device.

v0:
```python
import jax
import jax.numpy as jnp
from jax import lax
from jax.sharding import Mesh
from jax.sharding import PartitionSpec as P

HEADS = 8
HEAD_DIM = 64
SNAP = ("snap_0", "snap_1")
NODE_SNAP = ("node", "snap_0", "snap_1")


def from_behind(block, axis, distance):
    devices = range(lax.axis_size(axis))
    route = [(i - distance, i) for i in devices if i - distance in devices]
    return lax.ppermute(block, axis, route)


def in_blocks(value, dim, size):
    before, after = (value.shape[:dim], value.shape[dim + 1 :])
    return jnp.moveaxis(value.reshape(*before, size, -1, *after), dim, 0)


def joined_along(pieces, dim):
    shape = list(pieces.shape[1:])
    shape[dim] *= pieces.shape[0]
    return jnp.moveaxis(pieces, 0, dim).reshape(shape)


def exchange_in_order(pieces, axes, order):
    shape = [lax.axis_size(a) for a in axes]
    pieces = pieces.reshape(*shape, *pieces.shape[1:])
    for k in order:
        pieces = lax.all_to_all(pieces, axes[k], split_axis=k, concat_axis=k, tiled=True)
    return pieces.reshape(-1, *pieces.shape[len(axes) :])


def one_axis_at_a_time(value, axes, order, split_dim, concat_dim):
    pieces = in_blocks(value, split_dim, lax.axis_size(axes))
    return joined_along(exchange_in_order(pieces, axes, order), concat_dim)


def norm_rows(hidden, norm_gain):
    value = hidden.astype(jnp.float32)
    mean = jnp.mean(value, axis=-1, keepdims=True)
    centred = value - mean
    variance = jnp.mean(centred * centred, axis=-1, keepdims=True)
    return (centred * lax.rsqrt(variance + 1e-05) * norm_gain).astype(jnp.bfloat16)


def project_all(normed, w_query, w_key, w_value):
    query = jnp.dot(normed, w_query, preferred_element_type=jnp.float32).astype(jnp.bfloat16)
    key = jnp.dot(normed, w_key, preferred_element_type=jnp.float32).astype(jnp.bfloat16)
    value = jnp.dot(normed, w_value, preferred_element_type=jnp.float32).astype(jnp.bfloat16)
    return (query, key, value)


def near_one(feats, offset):
    return from_behind(feats, "node", offset)


def relay_one(received, offset):
    return from_behind(received, "node", offset)


def local(
    features,
    tile_rows,
    tile_cols,
    tile_values,
    tile_count,
    w_graph,
    norm_gain,
    w_query,
    w_key,
    w_value,
    w_out,
):
    feats = features[0]
    nodes_dev, width = feats.shape
    tile = tile_values.shape[-1]
    blocks_dev = nodes_dev // tile
    here = lax.axis_index("node")
    lower = near_one(feats, 1)
    upper = near_one(feats, -1)
    window = jnp.concatenate([relay_one(lower, 1), lower, feats, upper, relay_one(upper, -1)], 0)
    window = window.reshape(5 * blocks_dev, tile, width)
    local_cols = tile_cols[0] - (here - 2) * blocks_dev
    picked = jnp.take(window, local_cols, axis=0)
    live = jnp.arange(tile_values.shape[1]) < tile_count[0, 0]
    masked = tile_values[0] * live[:, None, None].astype(jnp.bfloat16)
    prod = jnp.einsum("tij,tjd->tid", masked, picked, preferred_element_type=jnp.float32)
    local_rows = tile_rows[0] - here * blocks_dev
    select = (local_rows[None, :] == jnp.arange(blocks_dev)[:, None]).astype(jnp.float32)
    summed = jnp.einsum("bt,tid->bid", select, prod, precision=lax.Precision.HIGHEST)
    aggregated = summed.reshape(nodes_dev, width).astype(jnp.bfloat16)
    mixed = jnp.dot(aggregated, w_graph, preferred_element_type=jnp.float32)
    hidden = (feats.astype(jnp.float32) + jax.nn.relu(mixed)).astype(jnp.bfloat16)
    resident = one_axis_at_a_time(hidden[None], SNAP, (1, 0), 1, 0)
    snaps, nodes_here = (resident.shape[0], resident.shape[1])
    normed = norm_rows(resident, norm_gain).reshape(snaps * nodes_here, width)
    query, key, value = project_all(normed, w_query, w_key, w_value)
    query = query.reshape(snaps, nodes_here, HEADS, HEAD_DIM)
    key = key.reshape(snaps, nodes_here, HEADS, HEAD_DIM)
    value = value.reshape(snaps, nodes_here, HEADS, HEAD_DIM)
    scores = jnp.einsum(
        "snhd,unhd->nhsu", query, key, preferred_element_type=jnp.float32
    ) * HEAD_DIM ** (-0.5)
    later = jnp.arange(snaps)[:, None] >= jnp.arange(snaps)[None, :]
    scores = jnp.where(later, scores, jnp.float32(-1e30))
    weights = jax.nn.softmax(scores, axis=-1).astype(jnp.bfloat16)
    context = jnp.einsum("nhsu,unhd->snhd", weights, value, preferred_element_type=jnp.float32)
    context = context.astype(jnp.bfloat16).reshape(snaps * nodes_here, width)
    projected = jnp.dot(context, w_out, preferred_element_type=jnp.float32)
    result = resident.reshape(snaps * nodes_here, width).astype(jnp.float32) + projected
    return result.astype(jnp.bfloat16).reshape(snaps, nodes_here, width)


def solution(mesh):
    split = Mesh(mesh.devices.reshape(4, 2, mesh.shape["node"]), ("snap_0", "snap_1", "node"))
    in_specs = (
        P(SNAP, "node", None),
        P(SNAP, "node"),
        P(SNAP, "node"),
        P(SNAP, "node", None, None),
        P(SNAP, "node"),
        P(),
        P(),
        P(),
        P(),
        P(),
        P(),
    )
    out_specs = P(None, NODE_SNAP, None)
    return jax.shard_map(local, mesh=split, in_specs=in_specs, out_specs=out_specs, check_vma=False)
```

profile of v0, /device:TPU:25, one launch (start us, length us, event | category | flops | bytes accessed | tf_op | source)
XLA Modules:
  0.0 151.9 jit_solution(11202411679129184954)
XLA Ops:
  0.0 0.0 copy-start
  0.0 3.7 %collective-permute-start = (bf16[1024,512]{1,0:T(8,128)(2,1)}, bf16[1024,512]{1,0:T(8,128)(2,1)}, u32[]{:S(2)}, u32[]{:S(2)}) collective-permute-start(bf16[1024,512]{1,0:T(8,128)(2,1)} %bitcast.56), channel_id=1, source_target_pairs={{0,1},{1,2},{2,3},{3,4},{4,5},{5,6},{6,7},{7,8},{8,9},{9,10},{10,1... | collective-permute-start | bytes 3145736 | tf_op jit(solution)/shard_map/ppermute | solution.py:16
  3.7 9.7 %collective-permute-start.2 = (bf16[1024,512]{1,0:T(8,128)(2,1)}, bf16[1024,512]{1,0:T(8,128)(2,1)S(1)}, u32[]{:S(2)}, u32[]{:S(2)}) collective-permute-start(bf16[1024,512]{1,0:T(8,128)(2,1)} %bitcast.57), channel_id=1, source_target_pairs={{1,0},{2,1},{3,2},{4,3},{5,4},{6,5},{7,6},{8,7},{9,8},{10,9},{11,1... | collective-permute-start | bytes 3145736 | tf_op jit(solution)/shard_map/ppermute | solution.py:16
  13.4 21.3 %collective-permute-done = bf16[1024,512]{1,0:T(8,128)(2,1)} collective-permute-done((bf16[1024,512]{1,0:T(8,128)(2,1)}, bf16[1024,512]{1,0:T(8,128)(2,1)}, u32[]{:S(2)}, u32[]{:S(2)}) %collective-permute-start) | collective-permute-done | bytes 1048608 | tf_op jit(solution)/shard_map/ppermute | solution.py:16
  34.6 1.9 %collective-permute-start.1 = (bf16[1024,512]{1,0:T(8,128)(2,1)}, bf16[1024,512]{1,0:T(8,128)(2,1)}, u32[]{:S(2)}, u32[]{:S(2)}) collective-permute-start(bf16[1024,512]{1,0:T(8,128)(2,1)} %collective-permute-done), channel_id=1, source_target_pairs={{0,1},{1,2},{2,3},{3,4},{4,5},{5,6},{6,7},{7,8},{8,9},{9,10},{10,1... | collective-permute-start | bytes 3145736 | tf_op jit(solution)/shard_map/ppermute | solution.py:16
  36.5 0.7 fusion.35
  37.2 0.0 collective-permute-done.2
  37.2 5.5 %collective-permute-start.3 = (bf16[1024,512]{1,0:T(8,128)(2,1)S(1)}, bf16[1024,512]{1,0:T(8,128)(2,1)S(1)}, u32[]{:S(2)}, u32[]{:S(2)}) collective-permute-start(bf16[1024,512]{1,0:T(8,128)(2,1)S(1)} %collective-permute-done.2), channel_id=1, source_target_pairs={{1,0},{2,1},{3,2},{4,3},{5,4},{6,5},{7,6},{8,7},{9,8},{10,9},{11,1... | collective-permute-start | bytes 3145736 | tf_op jit(solution)/shard_map/ppermute | solution.py:16
  42.7 0.7 subtract_bitcast_fusion
  44.0 0.7 compare_and_fusion
  44.7 17.7 %collective-permute-done.1 = bf16[1024,512]{1,0:T(8,128)(2,1)} collective-permute-done((bf16[1024,512]{1,0:T(8,128)(2,1)}, bf16[1024,512]{1,0:T(8,128)(2,1)}, u32[]{:S(2)}, u32[]{:S(2)}) %collective-permute-start.1) | collective-permute-done | bytes 1048608 | tf_op jit(solution)/shard_map/ppermute | solution.py:16
  62.4 2.3 %constant_dynamic-update-slice_fusion.4 = bf16[5120,512]{1,0:T(8,128)(2,1)} fusion(bf16[1024,512]{1,0:T(8,128)(2,1)} %collective-permute-done.1), kind=kLoop, calls=%fused_computation.45 | loop fusion | bytes 2097152
  64.6 2.3 %constant_dynamic-update-slice_fusion.3 = bf16[5120,512]{1,0:T(8,128)(2,1)} fusion(bf16[5120,512]{1,0:T(8,128)(2,1)} %constant_dynamic-update-slice_fusion.4, bf16[1024,512]{1,0:T(8,128)(2,1)} %collective-permute-done), kind=kLoop, calls=%fused_computation.44 | loop fusion | bytes 2097152
  66.9 0.0 copy-done.2
  66.9 1.1 constant_dynamic-update-slice_fusion.2
  68.0 1.0 constant_dynamic-update-slice_fusion.1
  69.0 0.0 collective-permute-done.3
  69.0 1.0 constant_dynamic-update-slice_fusion
  70.1 5.3 %gather_fusion = bf16[28,128,512]{2,1,0:T(8,128)(2,1)} fusion(bf16[40,128,512]{2,1,0:T(8,128)(2,1)} %bitcast.6, s32[1024]{0:T(1024)S(1)} %pad_clamp_fusion), kind=kCustom, calls=%fused_computation | custom fusion | bytes 7340144 | tf_op jit(solution)/shard_map/jit(_take)/gather | solution.py:89
  75.4 3.2 %fusion.3 = f32[28,128,512]{2,1,0:T(8,128)S(1)} fusion(bf16[28,128,512]{2,1,0:T(8,128)(2,1)} %gather_fusion, pred[28]{0:T(512)(128)(4,1)S(1)} %get-tuple-element.7, bf16[1,28,128,128]{3,2,1,0:T(8,128)(2,1)S(1)} %copy-done.3, bf16[28]{0:T(256)(128)(2,1)S(1)} %get-tuple-element.8), kind=kOutput, calls=%fused_computation.4 | convolution fusion | flops 472055808 | bytes 11927636 | tf_op jit(solution)/shard_map/tij,tjd->tid/dot_general | solution.py:92
  78.6 6.9 %fusion.20 = bf16[8,128,512]{2,0,1:T(8,128)(2,1)S(1)} fusion(f32[28,128,512]{2,1,0:T(8,128)S(1)} %fusion.3, s32[28]{0:T(128)S(1)} %subtract_bitcast_fusion), kind=kOutput, calls=%fused_computation.25 | convolution fusion | flops 176685280 | bytes 8388720 | tf_op jit(solution)/shard_map/bt,tid->bid/dot_general | solution.py:95
  85.5 0.3 copy.38
  85.8 0.7 add_convert_fusion
  86.5 0.1 copy.39
  86.6 6.3 %all_to_all.10 = bf16[4,2,1,128,512]{4,3,0,2,1:T(8,128)(2,1)S(1)} all-to-all(bf16[4,2,1,128,512]{4,3,0,2,1:T(8,128)(2,1)S(1)} %copy.39), channel_id=1, replica_groups=mesh['snap_0'=4,'snap_1'=2,'node'=64] {'snap_1'}, dimensions={1} | all-to-all | bytes 2097152 | tf_op jit(solution)/shard_map/all_to_all | solution.py:34
  93.0 1.1 copy.40
  94.0 4.1 %all-to-all-start.1 = ((bf16[4,2,1,128,512]{4,3,1,2,0:T(8,128)(2,1)}), bf16[4,2,1,128,512]{4,3,1,2,0:T(8,128)(2,1)S(1)}, u32[]{:S(2)}, u32[]{:S(2)}) async-start(bf16[4,2,1,128,512]{4,3,1,2,0:T(8,128)(2,1)} %copy.40), calls=%async_computation.1 | async-start | bytes 2097152 | tf_op jit(solution)/shard_map/all_to_all | solution.py:34
  98.2 14.5 %all-to-all-done.1 = bf16[4,2,1,128,512]{4,3,1,2,0:T(8,128)(2,1)S(1)} async-done(((bf16[4,2,1,128,512]{4,3,1,2,0:T(8,128)(2,1)}), bf16[4,2,1,128,512]{4,3,1,2,0:T(8,128)(2,1)S(1)}, u32[]{:S(2)}, u32[]{:S(2)}) %all-to-all-start.1) | async-done | bytes 1048608 | tf_op jit(solution)/shard_map/all_to_all | solution.py:34
  112.7 0.2 convert_reduce_fusion
  112.9 0.5 fusion.12
  113.5 0.4 fusion.15
  113.9 0.0 copy-start.1
  113.9 1.0 copy-done.1
  114.9 0.7 convolution_convert_fusion.1
  115.6 0.0 copy-start.6
  115.6 2.1 %reshape.112 = bf16[8,128,8,64]{3,2,1,0:T(8,128)(2,1)} reshape(bf16[1024,512]{1,0:T(8,128)(2,1)S(1)} %convolution_convert_fusion.1) | data formatting | bytes 2097152 | tf_op jit(solution)/shard_map/reshape | solution.py:103
  117.7 1.9 %convolution_convert_fusion = bf16[1024,512]{1,0:T(8,128)(2,1)S(1)} fusion(bf16[1024,512]{1,0:T(8,128)(2,1)} %copy-done.1, bf16[512,512]{1,0:T(8,128)(2,1)S(1)} %copy-done.6), kind=kOutput, calls=%fused_computation.26 | convolution fusion | flops 537395200 | bytes 2621440 | tf_op jit(solution)/shard_map/dot_general | solution.py:53
  119.6 2.1 %reshape.113 = bf16[8,128,8,64]{3,2,1,0:T(8,128)(2,1)} reshape(bf16[1024,512]{1,0:T(8,128)(2,1)S(1)} %convolution_convert_fusion) | data formatting | bytes 2097152 | tf_op jit(solution)/shard_map/reshape | solution.py:104
  121.7 6.7 %fusion.6 = f32[128,8,8,8]{2,3,1,0:T(8,128)} fusion(bf16[8,128,8,64]{3,2,1,0:T(8,128)(2,1)} %reshape.113, bf16[8,128,8,64]{3,2,1,0:T(8,128)(2,1)} %reshape.112), kind=kOutput, calls=%fused_computation.7 | convolution fusion | flops 8388608 | bytes 2359296 | tf_op jit(solution)/shard_map/snhd,unhd->nhsu/dot_general | solution.py:106
  128.4 3.8 %copy.46 = f32[128,8,8,8]{0,3,2,1:T(8,128)S(1)} copy(f32[128,8,8,8]{2,3,1,0:T(8,128)} %fusion.6) | data formatting | bytes 524288 | tf_op jit(solution)/shard_map/snhd,unhd->nhsu/dot_general | solution.py:106
  132.2 0.9 fusion.39
  133.1 3.7 %copy.48 = bf16[128,8,8,8]{3,2,1,0:T(8,128)(2,1)} copy(bf16[128,8,8,8]{0,3,2,1:T(8,128)(2,1)S(1)} %divide_convert_fusion) | data formatting | bytes 262144 | tf_op jit(solution)/shard_map/convert_element_type | solution.py:111
  136.9 1.9 %convolution_convert_fusion.2 = bf16[1024,512]{1,0:T(8,128)(2,1)S(1)} fusion(bf16[1024,512]{1,0:T(8,128)(2,1)} %copy-done.1, bf16[512,512]{1,0:T(8,128)(2,1)S(1)} %copy-done.7), kind=kOutput, calls=%fused_computation.28 | convolution fusion | flops 537395200 | bytes 2621440 | tf_op jit(solution)/shard_map/dot_general | solution.py:54
  138.8 2.1 %reshape.111 = bf16[8,128,8,64]{3,2,1,0:T(8,128)(2,1)} reshape(bf16[1024,512]{1,0:T(8,128)(2,1)S(1)} %convolution_convert_fusion.2) | data formatting | bytes 2097152 | tf_op jit(solution)/shard_map/reshape | solution.py:105
  140.9 5.2 %convert_bitcast_fusion = bf16[8,128,8,64]{3,0,2,1:T(8,128)(2,1)} fusion(bf16[128,8,8,8]{3,2,1,0:T(8,128)(2,1)} %copy.48, bf16[8,128,8,64]{3,2,1,0:T(8,128)(2,1)} %reshape.111), kind=kOutput, calls=%fused_computation.22 | convolution fusion | flops 8912896 | bytes 2228224 | tf_op jit(solution)/shard_map/nhsu,unhd->snhd/dot_general | solution.py:112
  146.1 4.1 %copy.49 = bf16[8,128,8,64]{1,0,3,2:T(8,128)(2,1)S(1)} copy(bf16[8,128,8,64]{3,0,2,1:T(8,128)(2,1)} %convert_bitcast_fusion) | data formatting | bytes 2097152 | tf_op jit(solution)/shard_map/convert_element_type | solution.py:113
  150.2 0.0 copy-done.8
  150.2 1.7 %fusion.16 = bf16[1024,512]{1,0:T(8,128)(2,1)} fusion(bf16[4,2,1,128,512]{4,3,1,2,0:T(8,128)(2,1)S(1)} %all-to-all-done.1, bf16[512,512]{1,0:T(8,128)(2,1)S(1)} %copy-done.8, bf16[64,8,8,128]{3,2,1,0:T(8,128)(2,1)S(1)} %bitcast.55), kind=kOutput, calls=%fused_computation.21 | convolution fusion | flops 538443776 | bytes 3670016 | tf_op jit(solution)/shard_map/dot_general | solution.py:114
  (17 shorter events, 0.1 us)
Async XLA Ops:
  0.0 85.8 %copy-start = (bf16[512,512]{1,0:T(8,128)(2,1)S(1)}, bf16[512,512]{1,0:T(8,128)(2,1)}, u32[]{:S(2)}) copy-start(bf16[512,512]{1,0:T(8,128)(2,1)} %param.16) | copy-start | bytes 1572868
  0.0 34.6 %collective-permute-start = (bf16[1024,512]{1,0:T(8,128)(2,1)}, bf16[1024,512]{1,0:T(8,128)(2,1)}, u32[]{:S(2)}, u32[]{:S(2)}) collective-permute-start(bf16[1024,512]{1,0:T(8,128)(2,1)} %bitcast.56), channel_id=1, source_target_pairs={{0,1},{1,2},{2,3},{3,4},{4,5},{5,6},{6,7},{7,8},{8,9},{9,10},{10,1... | collective-permute-start | bytes 3145736 | tf_op jit(solution)/shard_map/ppermute | solution.py:16
  3.7 33.5 %collective-permute-start.2 = (bf16[1024,512]{1,0:T(8,128)(2,1)}, bf16[1024,512]{1,0:T(8,128)(2,1)S(1)}, u32[]{:S(2)}, u32[]{:S(2)}) collective-permute-start(bf16[1024,512]{1,0:T(8,128)(2,1)} %bitcast.57), channel_id=1, source_target_pairs={{1,0},{2,1},{3,2},{4,3},{5,4},{6,5},{7,6},{8,7},{9,8},{10,9},{11,1... | collective-permute-start | bytes 3145736 | tf_op jit(solution)/shard_map/ppermute | solution.py:16
  34.6 27.7 %collective-permute-start.1 = (bf16[1024,512]{1,0:T(8,128)(2,1)}, bf16[1024,512]{1,0:T(8,128)(2,1)}, u32[]{:S(2)}, u32[]{:S(2)}) collective-permute-start(bf16[1024,512]{1,0:T(8,128)(2,1)} %collective-permute-done), channel_id=1, source_target_pairs={{0,1},{1,2},{2,3},{3,4},{4,5},{5,6},{6,7},{7,8},{8,9},{9,10},{10,1... | collective-permute-start | bytes 3145736 | tf_op jit(solution)/shard_map/ppermute | solution.py:16
  37.2 31.8 %collective-permute-start.3 = (bf16[1024,512]{1,0:T(8,128)(2,1)S(1)}, bf16[1024,512]{1,0:T(8,128)(2,1)S(1)}, u32[]{:S(2)}, u32[]{:S(2)}) collective-permute-start(bf16[1024,512]{1,0:T(8,128)(2,1)S(1)} %collective-permute-done.2), channel_id=1, source_target_pairs={{1,0},{2,1},{3,2},{4,3},{5,4},{6,5},{7,6},{8,7},{9,8},{10,9},{11,1... | collective-permute-start | bytes 3145736 | tf_op jit(solution)/shard_map/ppermute | solution.py:16
  44.7 22.3 %copy-start.2 = (bf16[1,1024,512]{2,1,0:T(8,128)(2,1)S(1)}, bf16[1,1024,512]{2,1,0:T(8,128)(2,1)}, u32[]{:S(2)}) copy-start(bf16[1,1024,512]{2,1,0:T(8,128)(2,1)} %param.11) | copy-start | bytes 3145732
  70.1 5.3 %copy-start.3 = (bf16[1,28,128,128]{3,2,1,0:T(8,128)(2,1)S(1)}, bf16[1,28,128,128]{3,2,1,0:T(8,128)(2,1)}, u32[]{:S(2)}) copy-start(bf16[1,28,128,128]{3,2,1,0:T(8,128)(2,1)} %param.14) | copy-start | bytes 2752516
  94.0 19.4 %copy-start.4 = (f32[512]{0:T(512)S(1)}, f32[512]{0:T(512)}, u32[]{:S(2)}) copy-start(f32[512]{0:T(512)} %param.17) | copy-start | bytes 6148
  94.0 18.7 %all-to-all-start.1 = ((bf16[4,2,1,128,512]{4,3,1,2,0:T(8,128)(2,1)}), bf16[4,2,1,128,512]{4,3,1,2,0:T(8,128)(2,1)S(1)}, u32[]{:S(2)}, u32[]{:S(2)}) async-start(bf16[4,2,1,128,512]{4,3,1,2,0:T(8,128)(2,1)} %copy.40), calls=%async_computation.1 | async-start | bytes 2097152 | tf_op jit(solution)/shard_map/all_to_all | solution.py:34
  98.2 16.7 %copy-start.5 = (bf16[512,512]{1,0:T(8,128)(2,1)S(1)}, bf16[512,512]{1,0:T(8,128)(2,1)}, u32[]{:S(2)}) copy-start(bf16[512,512]{1,0:T(8,128)(2,1)} %param.18) | copy-start | bytes 1572868
  113.9 1.0 copy-start.1
  115.6 2.1 %copy-start.6 = (bf16[512,512]{1,0:T(8,128)(2,1)S(1)}, bf16[512,512]{1,0:T(8,128)(2,1)}, u32[]{:S(2)}) copy-start(bf16[512,512]{1,0:T(8,128)(2,1)} %param.19) | copy-start | bytes 1572868
  132.2 4.7 %copy-start.7 = (bf16[512,512]{1,0:T(8,128)(2,1)S(1)}, bf16[512,512]{1,0:T(8,128)(2,1)}, u32[]{:S(2)}) copy-start(bf16[512,512]{1,0:T(8,128)(2,1)} %param.20) | copy-start | bytes 1572868
  146.1 4.1 %copy-start.8 = (bf16[512,512]{1,0:T(8,128)(2,1)S(1)}, bf16[512,512]{1,0:T(8,128)(2,1)}, u32[]{:S(2)}) copy-start(bf16[512,512]{1,0:T(8,128)(2,1)} %param.21) | copy-start | bytes 1572868
where the time goes:
time: 153 us; the launch traced here: 152 us
  waiting for transfers between devices  53.5 us (35%)
  local copies, waits for them, and re-layouts  33.4 us (22%)
  matrix products  28.9 us (19%)
  starting transfers between devices  24.9 us (16%)
  blocking collectives  6.35 us (4%)
  other arithmetic  4.07 us (3%)
    ppermute x4, waiting for transfers between devices, from_behind(): return lax.ppermute(block, axis, route)  38.9 us
    ppermute x4, starting transfers between devices, from_behind(): return lax.ppermute(block, axis, route)  20.7 us
    all_to_all x1, waiting for transfers between devices, exchange_in_order(): lax.all_to_all(pieces, axes[k], split_axis=k, concat_axis=k, tiled=True)  14.5 us
    unnamed x22, local copies, waits for them, and re-layouts  7.68 us
    dot_general x1, matrix products, local(): jnp.einsum('bt,tid->bid', select, prod, precision=lax.Precision.HIGHEST)  6.9 us
    dot_general x1, matrix products, local(): jnp.einsum('snhd,unhd->nhsu', query, key, preferred_element_type=jnp.floa...  6.68 us
    all_to_all x1, blocking collectives, exchange_in_order(): lax.all_to_all(pieces, axes[k], split_axis=k, concat_axis=k, tiled=True)  6.35 us
    gather x1, local copies, waits for them, and re-layouts, local(): picked = jnp.take(window, local_cols, axis=0)  5.27 us
  transfers between devices with their start and end apart: 5, of which 3 were waited for; matrix products, arithmetic and copies ran while one was open for 6% of the time, Pallas kernels for 0%

commit v1 on v0

v1 whole, which is shorter than its diff:
```python
import jax
import jax.numpy as jnp
from jax import lax
from jax.experimental import pallas as pl
from jax.experimental.pallas import tpu as pltpu
from jax.sharding import PartitionSpec as P

MESH = pl.DeviceIdType.MESH
HEADS = 8
HEAD_DIM = 64
LANES = 128
BF16 = jnp.bfloat16
F32 = jnp.float32


def layer_kernel(
    snaps,
    ring,
    rows_ref,
    cols_ref,
    count_ref,
    feat,
    tiles_hbm,
    wg_hbm,
    gain_hbm,
    wq_hbm,
    wk_hbm,
    wv_hbm,
    wo_hbm,
    out,
    win_a,
    win_b,
    win_c,
    win_d,
    tiles,
    part,
    aggregated,
    resident_agg,
    resident_feat,
    mixed,
    hidden,
    query,
    key,
    value,
    wg,
    gain,
    wqkv,
    wo,
    gather_heads,
    spread_heads,
    out_buf,
    prev_ref,
    last_ref,
    own_send,
    own_recv,
    relay_send,
    relay_recv,
    feat_send,
    feat_recv,
    agg_send,
    agg_recv,
    local_sem,
    out_sem,
):
    win = (win_a, win_b, win_c, win_d)
    blocks = feat.shape[0]
    tile = feat.shape[1]
    width = feat.shape[2]
    chunks = width // LANES
    slots = tiles.shape[0]
    s = lax.axis_index("snap")
    j = lax.axis_index("node")
    right = lax.rem(j + 1, ring)
    left = lax.rem(j + ring - 1, ring)
    node_peer = (right, left)
    near = (blocks, 3 * blocks)
    far = (0, 4 * blocks)

    def cols_of(c):
        return pl.ds(c * LANES, LANES)

    local = [pltpu.make_async_copy(tiles_hbm, tiles, local_sem.at[0])]
    for c in range(chunks):
        local.append(
            pltpu.make_async_copy(
                feat.at[:, :, cols_of(c)], win[c].at[pl.ds(2 * blocks, blocks)], local_sem.at[1 + c]
            )
        )
    base = 1 + chunks
    weights = [
        pltpu.make_async_copy(wg_hbm, wg, local_sem.at[base]),
        pltpu.make_async_copy(gain_hbm, gain, local_sem.at[base + 1]),
        pltpu.make_async_copy(wq_hbm, wqkv.at[0], local_sem.at[base + 2]),
        pltpu.make_async_copy(wk_hbm, wqkv.at[1], local_sem.at[base + 3]),
        pltpu.make_async_copy(wv_hbm, wqkv.at[2], local_sem.at[base + 4]),
        pltpu.make_async_copy(wo_hbm, wo, local_sem.at[base + 5]),
        pltpu.make_async_copy(feat.at[s], resident_feat.at[s], local_sem.at[base + 6]),
    ]

    def own(c, d):
        return pltpu.make_async_remote_copy(
            src_ref=feat.at[:, :, cols_of(c)],
            dst_ref=win[c].at[pl.ds(near[d], blocks)],
            send_sem=own_send.at[d, c],
            recv_sem=own_recv.at[d, c],
            device_id=(s, node_peer[d]),
            device_id_type=MESH,
        )

    def relay(c, d):
        return pltpu.make_async_remote_copy(
            src_ref=win[c].at[pl.ds(near[d], blocks)],
            dst_ref=win[c].at[pl.ds(far[d], blocks)],
            send_sem=relay_send.at[d, c],
            recv_sem=relay_recv.at[d, c],
            device_id=(s, node_peer[d]),
            device_id_type=MESH,
        )

    def feat_to(d):
        p = lax.rem(s + d, snaps)
        return pltpu.make_async_remote_copy(
            src_ref=feat.at[p],
            dst_ref=resident_feat.at[s],
            send_sem=feat_send.at[d - 1],
            recv_sem=feat_recv.at[d - 1],
            device_id=(p, j),
            device_id_type=MESH,
        )

    def agg_to(c, d):
        p = lax.rem(s + d, snaps)
        return pltpu.make_async_remote_copy(
            src_ref=aggregated.at[c, p],
            dst_ref=resident_agg.at[c, s],
            send_sem=agg_send.at[c, d - 1],
            recv_sem=agg_recv.at[c, d - 1],
            device_id=(p, j),
            device_id_type=MESH,
        )

    barrier = pltpu.get_barrier_semaphore()
    for d in range(2):
        pl.semaphore_signal(barrier, inc=1, device_id=(s, node_peer[d]), device_id_type=MESH)
    for d in range(1, snaps):
        pl.semaphore_signal(barrier, inc=1, device_id=(lax.rem(s + d, snaps), j), device_id_type=MESH)
    for copy in local:
        copy.start()
    pl.semaphore_wait(barrier, 1 + snaps)

    for c in range(2):
        for d in range(2):
            own(c, d).start()
    for copy in weights:
        copy.start()
    for d in range(1, snaps):
        feat_to(d).start()

    live_slots = count_ref[0, 0]

    def link(t, last):
        row = rows_ref[0, t] - j * blocks
        before = jnp.int32(0)
        for r in range(blocks):
            before = jnp.where(row == r, last[r], before)
        prev_ref[t] = before
        live = t < live_slots
        return tuple(jnp.where((row == r) & live, t + 1, last[r]) for r in range(blocks))

    last = lax.fori_loop(0, slots, link, (jnp.int32(0),) * blocks)
    for r in range(blocks):
        last_ref[r] = last[r]

    feature = lax.broadcasted_iota(jnp.int32, (width, LANES), 0) // HEAD_DIM
    lane = lax.broadcasted_iota(jnp.int32, (width, LANES), 1)
    for u in range(snaps):
        hit = lax.rem(lane, snaps * HEADS) == u * HEADS + feature
        gather_heads[u] = jnp.where(hit, HEAD_DIM**-0.5, 0.0).astype(BF16)
    feature = lax.broadcasted_iota(jnp.int32, (LANES, width), 1) // HEAD_DIM
    lane = lax.broadcasted_iota(jnp.int32, (LANES, width), 0)
    for u in range(snaps):
        spread_heads[u] = jnp.where(lane == u * HEADS + feature, 1.0, 0.0).astype(BF16)
    part[0] = jnp.zeros((tile, LANES), F32)

    def aggregate(c):
        def product(t, carry):
            column = jnp.clip(cols_ref[0, t] - (j - 2) * blocks, 0, 5 * blocks - 1)
            part[t + 1] = jnp.dot(tiles[t], win[c][column], preferred_element_type=F32)
            return carry

        def step(i, carry):
            for k in range(4):
                product(i * 4 + k, carry)
            return carry

        lax.fori_loop(0, slots // 4, step, 0)
        for t in range(slots // 4 * 4, slots):
            product(t, 0)

        def chain(t, carry):
            part[t + 1] = part[t + 1] + part[prev_ref[t]]
            return carry

        lax.fori_loop(0, slots, chain, 0)
        for r in range(blocks):
            aggregated[c, r] = part[last_ref[r]].astype(BF16)
        for d in range(1, snaps):
            agg_to(c, d).start()
        resident_agg[c, s] = aggregated[c, s]

    for copy in local:
        copy.wait()

    def pass_on(c):
        for d in range(2):
            own(c, d).wait_recv()
            relay(c, d).start()
            if c + 2 < chunks:
                own(c + 2, d).start()

    def arrived(c):
        for d in range(2):
            relay(c, d).wait_recv()

    pass_on(0)
    pass_on(1)
    for c in range(chunks):
        arrived(c)
        aggregate(c)
        if c + 2 < chunks:
            pass_on(c + 2)
        if c == chunks - 2:
            for copy in weights:
                copy.wait()
            for c2 in range(2):
                for d in range(1, snaps):
                    agg_to(c2, d).wait_recv()
            for u in range(snaps):
                pair = jnp.concatenate([resident_agg[0, u], resident_agg[1, u]], axis=1)
                mixed[u] = jnp.dot(pair, wg[pl.ds(0, 2 * LANES)], preferred_element_type=F32)

    for d in range(1, snaps):
        feat_to(d).wait_recv()
    for c2 in range(2, chunks):
        for d in range(1, snaps):
            agg_to(c2, d).wait_recv()

    lane = lax.broadcasted_iota(jnp.int32, (tile, LANES), 1)
    lane_snap = lax.rem(lane, snaps * HEADS) // HEADS
    period = snaps * HEADS
    for t in range(snaps):
        pair = jnp.concatenate([resident_agg[2, t], resident_agg[3, t]], axis=1)
        total = mixed[t] + jnp.dot(pair, wg[pl.ds(2 * LANES, 2 * LANES)], preferred_element_type=F32)
        hid = (resident_feat[t].astype(F32) + jnp.maximum(total, 0.0)).astype(BF16)
        hidden[t] = hid
        hid = hid.astype(F32)
        mean = jnp.mean(hid, axis=-1, keepdims=True)
        centred = hid - mean
        variance = jnp.mean(centred * centred, axis=-1, keepdims=True)
        normed = (centred * lax.rsqrt(variance + 1e-05) * gain[...]).astype(BF16)
        query[t] = jnp.dot(normed, wqkv[0], preferred_element_type=F32).astype(BF16)
        key[t] = jnp.dot(normed, wqkv[1], preferred_element_type=F32).astype(BF16)
        value[t] = jnp.dot(normed, wqkv[2], preferred_element_type=F32).astype(BF16)

    for t in range(snaps):
        q = query[t]
        scores = jnp.zeros((tile, LANES), F32)
        for u in range(t + 1):
            scores = scores + jnp.dot(q * key[u], gather_heads[u], preferred_element_type=F32)
        scores = jnp.where(lane_snap <= t, scores, -1e30)
        top = scores
        shift = HEADS
        while shift < period:
            top = jnp.maximum(top, pltpu.roll(top, shift, 1))
            shift *= 2
        e = jnp.exp(scores - top)
        total = e
        shift = HEADS
        while shift < period:
            total = total + pltpu.roll(total, shift, 1)
            shift *= 2
        w = (e / total).astype(BF16)
        context = jnp.zeros((tile, width), F32)
        for u in range(t + 1):
            wide = jnp.dot(w, spread_heads[u], preferred_element_type=F32)
            context = context + wide * value[u].astype(F32)
        projected = jnp.dot(context.astype(BF16), wo[...], preferred_element_type=F32)
        out_buf[t] = (hidden[t].astype(F32) + projected).astype(BF16)
        pltpu.make_async_copy(out_buf.at[t], out.at[t], out_sem.at[t]).start()

    for c in range(chunks):
        for d in range(2):
            own(c, d).wait_send()
            relay(c, d).wait_send()
        for d in range(1, snaps):
            agg_to(c, d).wait_send()
    for d in range(1, snaps):
        feat_to(d).wait_send()
    for t in range(snaps):
        pltpu.make_async_copy(out_buf.at[t], out.at[t], out_sem.at[t]).wait()


def local_layer(
    snaps,
    ring,
    features,
    tile_rows,
    tile_cols,
    tile_values,
    tile_count,
    w_graph,
    norm_gain,
    w_query,
    w_key,
    w_value,
    w_out,
):
    nodes_dev, width = features.shape[1:]
    slots, tile = tile_values.shape[1:3]
    blocks = nodes_dev // tile
    chunks = width // LANES
    smem = pl.BlockSpec(memory_space=pltpu.SMEM)
    anywhere = pl.BlockSpec(memory_space=pl.ANY)
    dma = pltpu.SemaphoreType.DMA

    def kernel(*refs):
        layer_kernel(snaps, ring, *refs)

    return pl.pallas_call(
        kernel,
        out_shape=jax.ShapeDtypeStruct((snaps, tile, width), BF16),
        in_specs=[smem] * 3 + [anywhere] * 8,
        out_specs=anywhere,
        scratch_shapes=[
            *[pltpu.VMEM((5 * blocks, tile, LANES), BF16)] * chunks,
            pltpu.VMEM((slots, tile, tile), BF16),
            pltpu.VMEM((slots + 1, tile, LANES), F32),
            pltpu.VMEM((chunks, blocks, tile, LANES), BF16),
            pltpu.VMEM((chunks, snaps, tile, LANES), BF16),
            pltpu.VMEM((snaps, tile, width), BF16),
            pltpu.VMEM((snaps, tile, width), F32),
            pltpu.VMEM((snaps, tile, width), BF16),
            pltpu.VMEM((snaps, tile, width), BF16),
            pltpu.VMEM((snaps, tile, width), BF16),
            pltpu.VMEM((snaps, tile, width), BF16),
            pltpu.VMEM((width, width), BF16),
            pltpu.VMEM((1, width), F32),
            pltpu.VMEM((3, width, width), BF16),
            pltpu.VMEM((width, width), BF16),
            pltpu.VMEM((snaps, width, LANES), BF16),
            pltpu.VMEM((snaps, LANES, width), BF16),
            pltpu.VMEM((snaps, tile, width), BF16),
            pltpu.SMEM((slots,), jnp.int32),
            pltpu.SMEM((blocks,), jnp.int32),
            dma((2, chunks)),
            dma((2, chunks)),
            dma((2, chunks)),
            dma((2, chunks)),
            dma((snaps - 1,)),
            dma((snaps - 1,)),
            dma((chunks, snaps - 1)),
            dma((chunks, snaps - 1)),
            dma((8 + chunks,)),
            dma((snaps,)),
        ],
        compiler_params=pltpu.CompilerParams(
            collective_id=0, has_side_effects=True, vmem_limit_bytes=48 * 2**20
        ),
        cost_estimate=pl.CostEstimate(
            flops=4 * 10**9, bytes_accessed=6 * 2**20, transcendentals=10**6
        ),
    )(
        tile_rows,
        tile_cols,
        tile_count,
        features.reshape(blocks, tile, width),
        tile_values[0],
        w_graph,
        norm_gain.reshape(1, width),
        w_query,
        w_key,
        w_value,
        w_out,
    )


def solution(mesh):
    snaps, ring = mesh.shape["snap"], mesh.shape["node"]

    def local(*args):
        return local_layer(snaps, ring, *args)

    in_specs = (
        P("snap", "node", None),
        P("snap", "node"),
        P("snap", "node"),
        P("snap", "node", None, None),
        P("snap", "node"),
        P(),
        P(),
        P(),
        P(),
        P(),
        P(),
    )
    return jax.shard_map(
        local, mesh=mesh, in_specs=in_specs, out_specs=P(None, ("node", "snap"), None), check_vma=False
    )
```

time: 153 us -> 96.1 us (0.63)
  the two profiles are of different devices: /device:TPU:25 before, /device:TPU:1 now
where the time goes in v1:
time: 96.1 us; the launch traced here: 95.6 us
  Pallas kernels  85.7 us (89%)
  local copies, waits for them, and re-layouts  9.24 us (10%)
    pallas_call x1, Pallas kernels, local_layer(): pl.pallas_call(kernel, out_shape=jax.ShapeDtypeStruct((snaps, tile, width...  85.7 us
    unnamed x21, local copies, waits for them, and re-layouts  9.24 us

profile of v1, /device:TPU:1, one launch (start us, length us, event | category | flops | bytes accessed | tf_op | source)
XLA Modules:
  0.0 95.6 jit_solution(188415630065712047)
XLA Ops:
  0.7 0.0 copy-start.7
  0.7 0.0 copy-start.8
  0.7 0.0 copy-start.9
  0.7 0.7 copy-done.7
  1.3 0.0 copy-done.8
  1.3 0.0 copy-done.9
  1.3 0.0 copy-start
  1.3 1.2 %copy-done = bf16[1,1024,512]{2,1,0:T(8,128)(2,1)S(1)} copy-done((bf16[1,1024,512]{2,1,0:T(8,128)(2,1)S(1)}, bf16[1,1024,512]{2,1,0:T(8,128)(2,1)}, u32[]{:S(2)}) %copy-start) | copy-done | bytes 1048600
  2.6 0.0 copy-start.1
  2.6 1.2 %copy-done.1 = bf16[1,28,128,128]{3,2,1,0:T(8,128)(2,1)S(1)} copy-done((bf16[1,28,128,128]{3,2,1,0:T(8,128)(2,1)S(1)}, bf16[1,28,128,128]{3,2,1,0:T(8,128)(2,1)}, u32[]{:S(2)}) %copy-start.1) | copy-done | bytes 917528
  3.7 0.0 copy-start.2
  3.7 1.0 %copy-done.2 = bf16[512,512]{1,0:T(8,128)(2,1)S(1)} copy-done((bf16[512,512]{1,0:T(8,128)(2,1)S(1)}, bf16[512,512]{1,0:T(8,128)(2,1)}, u32[]{:S(2)}) %copy-start.2) | copy-done | bytes 524312
  4.8 0.0 copy-start.3
  4.8 1.0 %copy-done.3 = bf16[512,512]{1,0:T(8,128)(2,1)S(1)} copy-done((bf16[512,512]{1,0:T(8,128)(2,1)S(1)}, bf16[512,512]{1,0:T(8,128)(2,1)}, u32[]{:S(2)}) %copy-start.3) | copy-done | bytes 524312
  5.8 0.0 copy-start.4
  5.8 1.0 %copy-done.4 = bf16[512,512]{1,0:T(8,128)(2,1)S(1)} copy-done((bf16[512,512]{1,0:T(8,128)(2,1)S(1)}, bf16[512,512]{1,0:T(8,128)(2,1)}, u32[]{:S(2)}) %copy-start.4) | copy-done | bytes 524312
  6.9 0.0 copy-start.5
  6.9 1.0 %copy-done.5 = bf16[512,512]{1,0:T(8,128)(2,1)S(1)} copy-done((bf16[512,512]{1,0:T(8,128)(2,1)S(1)}, bf16[512,512]{1,0:T(8,128)(2,1)}, u32[]{:S(2)}) %copy-start.5) | copy-done | bytes 524312
  7.9 0.0 copy-start.6
  7.9 1.0 %copy-done.6 = bf16[512,512]{1,0:T(8,128)(2,1)S(1)} copy-done((bf16[512,512]{1,0:T(8,128)(2,1)S(1)}, bf16[512,512]{1,0:T(8,128)(2,1)}, u32[]{:S(2)}) %copy-start.6) | copy-done | bytes 524312
  9.0 85.7 %shard_map.109 = bf16[8,128,512]{2,1,0:T(8,128)(2,1)S(1)} custom-call(s32[1,28]{1,0:T(1,128)S(1)} %copy-done.8, s32[1,28]{1,0:T(1,128)S(1)} %copy-done.9, s32[1,1]{1,0:T(1,128)S(6)} %copy.13.refs_2_, bf16[8,128,512]{2,1,0:T(8,128)(2,1)S(1)} %bitcast.3, bf16[28,128,128]{2,1,0:T(8,128)(2,1)S(1)} %bitcast.4, bf16[512,512]{1,0:T(8,128)(2,1)S(1)} %copy-done.2, ...), custom_call_target="tpu_custom_call" | custom-call | flops 4000000000 | bytes 6291456 | tf_op jit(solution)/shard_map/pallas_call | solution.py:329
  94.6 1.0 %copy.14 = bf16[8,128,512]{2,1,0:T(8,128)(2,1)} copy(bf16[8,128,512]{2,1,0:T(8,128)(2,1)S(1)} %shard_map.109) | data formatting | bytes 2097152
Async XLA Ops:
  0.7 0.7 copy-start.7
  0.7 0.7 copy-start.8
  0.7 0.7 copy-start.9
  1.3 1.2 %copy-start = (bf16[1,1024,512]{2,1,0:T(8,128)(2,1)S(1)}, bf16[1,1024,512]{2,1,0:T(8,128)(2,1)}, u32[]{:S(2)}) copy-start(bf16[1,1024,512]{2,1,0:T(8,128)(2,1)} %param.11) | copy-start | bytes 3145732
  2.6 1.2 %copy-start.1 = (bf16[1,28,128,128]{3,2,1,0:T(8,128)(2,1)S(1)}, bf16[1,28,128,128]{3,2,1,0:T(8,128)(2,1)}, u32[]{:S(2)}) copy-start(bf16[1,28,128,128]{3,2,1,0:T(8,128)(2,1)} %param.14) | copy-start | bytes 2752516
  3.7 1.0 %copy-start.2 = (bf16[512,512]{1,0:T(8,128)(2,1)S(1)}, bf16[512,512]{1,0:T(8,128)(2,1)}, u32[]{:S(2)}) copy-start(bf16[512,512]{1,0:T(8,128)(2,1)} %refs_5_.1) | copy-start | bytes 1572868
  4.8 1.0 %copy-start.3 = (bf16[512,512]{1,0:T(8,128)(2,1)S(1)}, bf16[512,512]{1,0:T(8,128)(2,1)}, u32[]{:S(2)}) copy-start(bf16[512,512]{1,0:T(8,128)(2,1)} %refs_7_.1) | copy-start | bytes 1572868
  5.8 1.0 %copy-start.4 = (bf16[512,512]{1,0:T(8,128)(2,1)S(1)}, bf16[512,512]{1,0:T(8,128)(2,1)}, u32[]{:S(2)}) copy-start(bf16[512,512]{1,0:T(8,128)(2,1)} %refs_8_.1) | copy-start | bytes 1572868
  6.9 1.0 %copy-start.5 = (bf16[512,512]{1,0:T(8,128)(2,1)S(1)}, bf16[512,512]{1,0:T(8,128)(2,1)}, u32[]{:S(2)}) copy-start(bf16[512,512]{1,0:T(8,128)(2,1)} %refs_9_.1) | copy-start | bytes 1572868
  7.9 1.0 %copy-start.6 = (bf16[512,512]{1,0:T(8,128)(2,1)S(1)}, bf16[512,512]{1,0:T(8,128)(2,1)}, u32[]{:S(2)}) copy-start(bf16[512,512]{1,0:T(8,128)(2,1)} %refs_10_.1) | copy-start | bytes 1572868

commit v2 on v1

--- a/solution.py
+++ b/solution.py
@@ -48,6 +48,10 @@
     wo,
     gather_heads,
     spread_heads,
+    normed,
+    partial,
+    wide,
+    context,
     out_buf,
     prev_ref,
     last_ref,
@@ -67,6 +71,8 @@
     tile = feat.shape[1]
     width = feat.shape[2]
     chunks = width // LANES
+    group = LANES // HEADS
+    period = snaps * HEADS
     slots = tiles.shape[0]
     s = lax.axis_index("snap")
     j = lax.axis_index("node")
@@ -171,15 +177,26 @@
     for r in range(blocks):
         last_ref[r] = last[r]
 
-    feature = lax.broadcasted_iota(jnp.int32, (width, LANES), 0) // HEAD_DIM
-    lane = lax.broadcasted_iota(jnp.int32, (width, LANES), 1)
-    for u in range(snaps):
-        hit = lax.rem(lane, snaps * HEADS) == u * HEADS + feature
-        gather_heads[u] = jnp.where(hit, HEAD_DIM**-0.5, 0.0).astype(BF16)
-    feature = lax.broadcasted_iota(jnp.int32, (LANES, width), 1) // HEAD_DIM
-    lane = lax.broadcasted_iota(jnp.int32, (LANES, width), 0)
-    for u in range(snaps):
-        spread_heads[u] = jnp.where(lane == u * HEADS + feature, 1.0, 0.0).astype(BF16)
+    place = lax.broadcasted_iota(jnp.int32, (width, width), 1)
+    source = lax.broadcasted_iota(jnp.int32, (width, width), 0)
+    moved = lax.rem(place, HEADS) * HEAD_DIM + place // LANES * group + lax.rem(place, LANES) // HEADS
+    order = jnp.where(source == moved, 1.0, 0.0).astype(BF16)
+    moved = lax.rem(source, HEADS) * HEAD_DIM + source // LANES * group + lax.rem(source, LANES) // HEADS
+    order_back = jnp.where(place == moved, 1.0, 0.0).astype(BF16)
+    lane = lax.broadcasted_iota(jnp.int32, (snaps * LANES, LANES), 1)
+    row = lax.broadcasted_iota(jnp.int32, (snaps * LANES, LANES), 0)
+    hit = lax.rem(lane, period) == row // LANES * HEADS + lax.rem(row, HEADS)
+    gather_heads[...] = jnp.where(hit, HEAD_DIM**-0.5, 0.0).astype(BF16)
+    lane = lax.broadcasted_iota(jnp.int32, (LANES, snaps * LANES), 1)
+    row = lax.broadcasted_iota(jnp.int32, (LANES, snaps * LANES), 0)
+    hit = row == lane // LANES * HEADS + lax.rem(lane, HEADS)
+    spread_heads[...] = jnp.where(hit, 1.0, 0.0).astype(BF16)
+    partial[...] = jnp.zeros(partial.shape, BF16)
+    for copy in weights:
+        copy.wait()
+    for i in range(3):
+        wqkv[i] = jnp.dot(wqkv[i], order, preferred_element_type=F32).astype(BF16)
+    wo[...] = jnp.dot(order_back, wo[...], preferred_element_type=F32).astype(BF16)
     part[0] = jnp.zeros((tile, LANES), F32)
 
     def aggregate(c):
@@ -230,8 +247,6 @@
         if c + 2 < chunks:
             pass_on(c + 2)
         if c == chunks - 2:
-            for copy in weights:
-                copy.wait()
             for c2 in range(2):
                 for d in range(1, snaps):
                     agg_to(c2, d).wait_recv()
@@ -245,48 +260,79 @@
         for d in range(1, snaps):
             agg_to(c2, d).wait_recv()
 
-    lane = lax.broadcasted_iota(jnp.int32, (tile, LANES), 1)
-    lane_snap = lax.rem(lane, snaps * HEADS) // HEADS
-    period = snaps * HEADS
-    for t in range(snaps):
-        pair = jnp.concatenate([resident_agg[2, t], resident_agg[3, t]], axis=1)
-        total = mixed[t] + jnp.dot(pair, wg[pl.ds(2 * LANES, 2 * LANES)], preferred_element_type=F32)
-        hid = (resident_feat[t].astype(F32) + jnp.maximum(total, 0.0)).astype(BF16)
-        hidden[t] = hid
-        hid = hid.astype(F32)
-        mean = jnp.mean(hid, axis=-1, keepdims=True)
-        centred = hid - mean
-        variance = jnp.mean(centred * centred, axis=-1, keepdims=True)
-        normed = (centred * lax.rsqrt(variance + 1e-05) * gain[...]).astype(BF16)
-        query[t] = jnp.dot(normed, wqkv[0], preferred_element_type=F32).astype(BF16)
-        key[t] = jnp.dot(normed, wqkv[1], preferred_element_type=F32).astype(BF16)
-        value[t] = jnp.dot(normed, wqkv[2], preferred_element_type=F32).astype(BF16)
-
-    for t in range(snaps):
-        q = query[t]
-        scores = jnp.zeros((tile, LANES), F32)
-        for u in range(t + 1):
-            scores = scores + jnp.dot(q * key[u], gather_heads[u], preferred_element_type=F32)
-        scores = jnp.where(lane_snap <= t, scores, -1e30)
-        top = scores
-        shift = HEADS
-        while shift < period:
-            top = jnp.maximum(top, pltpu.roll(top, shift, 1))
-            shift *= 2
-        e = jnp.exp(scores - top)
-        total = e
-        shift = HEADS
-        while shift < period:
-            total = total + pltpu.roll(total, shift, 1)
-            shift *= 2
-        w = (e / total).astype(BF16)
-        context = jnp.zeros((tile, width), F32)
-        for u in range(t + 1):
-            wide = jnp.dot(w, spread_heads[u], preferred_element_type=F32)
-            context = context + wide * value[u].astype(F32)
-        projected = jnp.dot(context.astype(BF16), wo[...], preferred_element_type=F32)
-        out_buf[t] = (hidden[t].astype(F32) + projected).astype(BF16)
-        pltpu.make_async_copy(out_buf.at[t], out.at[t], out_sem.at[t]).start()
+    half = snaps // 2
+    rows = half * tile
+    for h in range(2):
+        for t in range(h * half, (h + 1) * half):
+            pair = jnp.concatenate([resident_agg[2, t], resident_agg[3, t]], axis=1)
+            total = mixed[t] + jnp.dot(pair, wg[pl.ds(2 * LANES, 2 * LANES)], preferred_element_type=F32)
+            hid = (resident_feat[t].astype(F32) + jnp.maximum(total, 0.0)).astype(BF16)
+            hidden[t] = hid
+            hid = hid.astype(F32)
+            mean = jnp.mean(hid, axis=-1, keepdims=True)
+            centred = hid - mean
+            variance = jnp.mean(centred * centred, axis=-1, keepdims=True)
+            normed[t] = (centred * lax.rsqrt(variance + 1e-05) * gain[...]).astype(BF16)
+        part_of = pl.ds(h * half, half)
+        some = normed[part_of].reshape(rows, width)
+        for i, to in enumerate((query, key, value)):
+            product = jnp.dot(some, wqkv[i], preferred_element_type=F32).astype(BF16).astype(F32)
+            to[part_of] = product.reshape(half, tile, width)
+
+    def column(u):
+        return pl.ds(u * LANES, LANES)
+
+    def score_rows(i, carry):
+        at = pl.ds(pl.multiple_of(i * 16, 16), 16)
+        for t in range(snaps):
+            for u in range(t + 1):
+                total = query[t, at, column(0)] * key[u, at, column(0)]
+                for v in range(1, chunks):
+                    total = total + query[t, at, column(v)] * key[u, at, column(v)]
+                partial[t, at, column(u)] = total.astype(BF16)
+        return carry
+
+    lax.fori_loop(0, tile // 16, score_rows, 0)
+
+    lane = lax.broadcasted_iota(jnp.int32, (snaps, tile, LANES), 2)
+    of_row = lax.broadcasted_iota(jnp.int32, (snaps, tile, LANES), 0)
+    visible = (lax.rem(lane, period) // HEADS <= of_row).reshape(snaps * tile, LANES)
+    scores = jnp.dot(
+        partial[...].reshape(snaps * tile, snaps * LANES), gather_heads[...], preferred_element_type=F32
+    )
+    scores = jnp.where(visible, scores, -1e30)
+    top = scores
+    shift = HEADS
+    while shift < period:
+        top = jnp.maximum(top, pltpu.roll(top, shift, 1))
+        shift *= 2
+    e = jnp.exp(scores - top)
+    total = e
+    shift = HEADS
+    while shift < period:
+        total = total + pltpu.roll(total, shift, 1)
+        shift *= 2
+    w = (e / total).astype(BF16)
+    wide[...] = jnp.dot(w, spread_heads[...], preferred_element_type=F32).reshape(wide.shape)
+
+    def context_rows(i, carry):
+        at = pl.ds(pl.multiple_of(i * 16, 16), 16)
+        for t in range(snaps):
+            for v in range(chunks):
+                total = wide[t, at, column(0)] * value[0, at, column(v)]
+                for u in range(1, t + 1):
+                    total = total + wide[t, at, column(u)] * value[u, at, column(v)]
+                context[t, at, column(v)] = total.astype(BF16)
+        return carry
+
+    lax.fori_loop(0, tile // 16, context_rows, 0)
+
+    for h in range(2):
+        part_of = pl.ds(h * half, half)
+        projected = jnp.dot(context[part_of].reshape(rows, width), wo[...], preferred_element_type=F32)
+        result = hidden[part_of].astype(F32) + projected.reshape(half, tile, width)
+        out_buf[part_of] = result.astype(BF16)
+        pltpu.make_async_copy(out_buf.at[part_of], out.at[part_of], out_sem.at[h]).start()
 
     for c in range(chunks):
         for d in range(2):
@@ -296,8 +342,9 @@
             agg_to(c, d).wait_send()
     for d in range(1, snaps):
         feat_to(d).wait_send()
-    for t in range(snaps):
-        pltpu.make_async_copy(out_buf.at[t], out.at[t], out_sem.at[t]).wait()
+    for h in range(2):
+        part_of = pl.ds(h * half, half)
+        pltpu.make_async_copy(out_buf.at[part_of], out.at[part_of], out_sem.at[h]).wait()
 
 
 def local_layer(
@@ -320,7 +367,7 @@
     blocks = nodes_dev // tile
     chunks = width // LANES
     smem = pl.BlockSpec(memory_space=pltpu.SMEM)
-    anywhere = pl.BlockSpec(memory_space=pl.ANY)
+    hbm = pl.BlockSpec(memory_space=pltpu.HBM)
     dma = pltpu.SemaphoreType.DMA
 
     def kernel(*refs):
@@ -329,8 +376,8 @@
     return pl.pallas_call(
         kernel,
         out_shape=jax.ShapeDtypeStruct((snaps, tile, width), BF16),
-        in_specs=[smem] * 3 + [anywhere] * 8,
-        out_specs=anywhere,
+        in_specs=[smem] * 3 + [hbm] * 8,
+        out_specs=hbm,
         scratch_shapes=[
             *[pltpu.VMEM((5 * blocks, tile, LANES), BF16)] * chunks,
             pltpu.VMEM((slots, tile, tile), BF16),
@@ -340,15 +387,19 @@
             pltpu.VMEM((snaps, tile, width), BF16),
             pltpu.VMEM((snaps, tile, width), F32),
             pltpu.VMEM((snaps, tile, width), BF16),
-            pltpu.VMEM((snaps, tile, width), BF16),
-            pltpu.VMEM((snaps, tile, width), BF16),
-            pltpu.VMEM((snaps, tile, width), BF16),
+            pltpu.VMEM((snaps, tile, width), F32),
+            pltpu.VMEM((snaps, tile, width), F32),
+            pltpu.VMEM((snaps, tile, width), F32),
             pltpu.VMEM((width, width), BF16),
             pltpu.VMEM((1, width), F32),
             pltpu.VMEM((3, width, width), BF16),
             pltpu.VMEM((width, width), BF16),
-            pltpu.VMEM((snaps, width, LANES), BF16),
-            pltpu.VMEM((snaps, LANES, width), BF16),
+            pltpu.VMEM((snaps * LANES, LANES), BF16),
+            pltpu.VMEM((LANES, snaps * LANES), BF16),
+            pltpu.VMEM((snaps, tile, width), BF16),
+            pltpu.VMEM((snaps, tile, snaps * LANES), BF16),
+            pltpu.VMEM((snaps, tile, snaps * LANES), F32),
+            pltpu.VMEM((snaps, tile, width), BF16),
             pltpu.VMEM((snaps, tile, width), BF16),
             pltpu.SMEM((slots,), jnp.int32),
             pltpu.SMEM((blocks,), jnp.int32),
@@ -364,7 +415,7 @@
             dma((snaps,)),
         ],
         compiler_params=pltpu.CompilerParams(
-            collective_id=0, has_side_effects=True, vmem_limit_bytes=48 * 2**20
+            collective_id=0, has_side_effects=True, vmem_limit_bytes=60 * 2**20
         ),
         cost_estimate=pl.CostEstimate(
             flops=4 * 10**9, bytes_accessed=6 * 2**20, transcendentals=10**6

time: 96.1 us -> 82.5 us (0.86)
  local copies, waits for them, and re-layouts: 9.24 us -> 2.26 us
  Pallas kernels: 85.7 us -> 79.4 us
    unnamed x21 -> x1, local copies, waits for them, and re-layouts: 9.24 us -> 2.26 us
    pallas_call x1, Pallas kernels: 85.7 us -> 79.4 us  [local_layer(): pl.pallas_call(kernel, out_shape=jax.ShapeDtypeStruct((snaps, tile, width...]
where the time goes in v2:
time: 82.5 us; the launch traced here: 82.3 us
  Pallas kernels  79.4 us (96%)
  local copies, waits for them, and re-layouts  2.26 us (3%)
    pallas_call x1, Pallas kernels, local_layer(): pl.pallas_call(kernel, out_shape=jax.ShapeDtypeStruct((snaps, tile, width...  79.4 us
    unnamed x1, local copies, waits for them, and re-layouts  2.26 us

profile of v2, /device:TPU:1, one launch (start us, length us, event | category | flops | bytes accessed | tf_op | source)
XLA Modules:
  0.0 82.3 jit_solution(16770082799242280438)
XLA Ops:
  0.7 79.4 %shard_map.109 = bf16[8,128,512]{2,1,0:T(8,128)(2,1)} custom-call(s32[1,28]{1,0:T(1,128)} %refs_0_.1, s32[1,28]{1,0:T(1,128)} %refs_1_.1, s32[1,1]{1,0:T(1,128)S(6)} %copy.13.refs_2_, bf16[8,128,512]{2,1,0:T(8,128)(2,1)} %bitcast.3, bf16[28,128,128]{2,1,0:T(8,128)(2,1)} %bitcast.4, bf16[512,512]{1,0:T(8,128)(2,1)} %refs_5_.1, f32[1,512]{1,0:T(1,128)} %bitcast.5, ...), custom_call_target="tpu_custom_call" | custom-call | flops 4000000000 | bytes 6291456 | tf_op jit(solution)/shard_map/pallas_call | solution.py:376
  80.0 2.3 %copy.14 = bf16[8,128,512]{2,1,0:T(8,128)(2,1)} copy(bf16[8,128,512]{2,1,0:T(8,128)(2,1)} %shard_map.109) | data formatting | bytes 2097152

commit v3 on v2

--- a/solution.py
+++ b/solution.py
@@ -48,12 +48,15 @@
     wo,
     gather_heads,
     spread_heads,
-    normed,
     partial,
     wide,
     context,
     out_buf,
-    prev_ref,
+    key_ref,
+    rank_ref,
+    slot_ref,
+    column_ref,
+    keep_ref,
     last_ref,
     own_send,
     own_recv,
@@ -79,6 +82,10 @@
     right = lax.rem(j + 1, ring)
     left = lax.rem(j + ring - 1, ring)
     node_peer = (right, left)
+    has_left, has_right = j > 0, j < ring - 1
+    has_both = has_left & has_right
+    sends, receives = (has_right, has_left), (has_left, has_right)
+    receives_far = (j > 1, j < ring - 2)
     near = (blocks, 3 * blocks)
     far = (0, 4 * blocks)
 
@@ -123,57 +130,111 @@
             device_id_type=MESH,
         )
 
-    def feat_to(d):
-        p = lax.rem(s + d, snaps)
+    def feat_with(p):
         return pltpu.make_async_remote_copy(
             src_ref=feat.at[p],
             dst_ref=resident_feat.at[s],
-            send_sem=feat_send.at[d - 1],
-            recv_sem=feat_recv.at[d - 1],
+            send_sem=feat_send.at[p],
+            recv_sem=feat_recv.at[s],
             device_id=(p, j),
             device_id_type=MESH,
         )
 
-    def agg_to(c, d):
-        p = lax.rem(s + d, snaps)
+    def feat_from(p):
+        return pltpu.make_async_remote_copy(
+            src_ref=feat.at[p],
+            dst_ref=resident_feat.at[p],
+            send_sem=feat_send.at[p],
+            recv_sem=feat_recv.at[p],
+            device_id=(p, j),
+            device_id_type=MESH,
+        )
+
+    def agg_with(c, p):
         return pltpu.make_async_remote_copy(
             src_ref=aggregated.at[c, p],
             dst_ref=resident_agg.at[c, s],
-            send_sem=agg_send.at[c, d - 1],
-            recv_sem=agg_recv.at[c, d - 1],
+            send_sem=agg_send.at[c, p],
+            recv_sem=agg_recv.at[c, s],
             device_id=(p, j),
             device_id_type=MESH,
         )
 
+    def agg_from(c, p):
+        return pltpu.make_async_remote_copy(
+            src_ref=aggregated.at[c, p],
+            dst_ref=resident_agg.at[c, p],
+            send_sem=agg_send.at[c, p],
+            recv_sem=agg_recv.at[c, p],
+            device_id=(p, j),
+            device_id_type=MESH,
+        )
+
+    chips = snaps // 2
+    chip = lax.div(s, 2)
+    other_core = s + 1 - 2 * lax.rem(s, 2)
+    pair_of = [2 * lax.rem(chip + g, chips) for g in range(chips)]
+    near_first = (0, 1, 3, 2)
+    peers = [pair_of[g] + k for g in (2, 1, 3) for k in range(2)] + [other_core]
+
     barrier = pltpu.get_barrier_semaphore()
     for d in range(2):
-        pl.semaphore_signal(barrier, inc=1, device_id=(s, node_peer[d]), device_id_type=MESH)
-    for d in range(1, snaps):
-        pl.semaphore_signal(barrier, inc=1, device_id=(lax.rem(s + d, snaps), j), device_id_type=MESH)
+
+        @pl.when(sends[d])
+        def _():
+            pl.semaphore_signal(barrier, inc=1, device_id=(s, node_peer[d]), device_id_type=MESH)
+
+    for p in peers:
+        pl.semaphore_signal(barrier, inc=1, device_id=(p, j), device_id_type=MESH)
     for copy in local:
         copy.start()
-    pl.semaphore_wait(barrier, 1 + snaps)
+    for copy in weights:
+        copy.start()
+    pl.semaphore_wait(
+        barrier, snaps - 1 + has_left.astype(jnp.int32) + has_right.astype(jnp.int32)
+    )
+
+    def start_own(c, d):
+        @pl.when(sends[d])
+        def _():
+            own(c, d).start()
 
     for c in range(2):
         for d in range(2):
-            own(c, d).start()
-    for copy in weights:
-        copy.start()
-    for d in range(1, snaps):
-        feat_to(d).start()
+            start_own(c, d)
+    for p in peers:
+        feat_with(p).start()
 
     live_slots = count_ref[0, 0]
 
-    def link(t, last):
-        row = rows_ref[0, t] - j * blocks
-        before = jnp.int32(0)
-        for r in range(blocks):
-            before = jnp.where(row == r, last[r], before)
-        prev_ref[t] = before
-        live = t < live_slots
-        return tuple(jnp.where((row == r) & live, t + 1, last[r]) for r in range(blocks))
-
-    last = lax.fori_loop(0, slots, link, (jnp.int32(0),) * blocks)
+    def find_key(t, carry):
+        key_ref[t] = jnp.where(t < live_slots, rows_ref[0, t] - j * blocks, blocks)
+        return carry
+
+    def find_rank(t, carry):
+        mine = key_ref[t]
+        rank = jnp.int32(0)
+        for o in range(slots):
+            theirs = key_ref[o]
+            ahead = (theirs < mine) | ((theirs == mine) & (o < t))
+            rank = rank + ahead.astype(jnp.int32)
+        rank_ref[t] = rank
+        return carry
+
+    def find_slot(p, last):
+        slot = jnp.int32(0)
+        for o in range(slots):
+            slot = jnp.where(rank_ref[o] == p, o, slot)
+        slot_ref[p] = slot
+        row = key_ref[slot]
+        column_ref[p] = jnp.clip(cols_ref[0, slot] - (j - 2) * blocks, 0, 5 * blocks - 1)
+        keep_ref[p] = jnp.where(row == last[blocks], 1.0, 0.0)
+        ends = tuple(jnp.where(row == r, p + 1, last[r]) for r in range(blocks))
+        return ends + (row,)
+
+    lax.fori_loop(0, slots, find_key, 0)
+    lax.fori_loop(0, slots, find_rank, 0)
+    last = lax.fori_loop(0, slots, find_slot, (jnp.int32(0),) * blocks + (jnp.int32(-1),))
     for r in range(blocks):
         last_ref[r] = last[r]
 
@@ -200,29 +261,24 @@
     part[0] = jnp.zeros((tile, LANES), F32)
 
     def aggregate(c):
-        def product(t, carry):
-            column = jnp.clip(cols_ref[0, t] - (j - 2) * blocks, 0, 5 * blocks - 1)
-            part[t + 1] = jnp.dot(tiles[t], win[c][column], preferred_element_type=F32)
-            return carry
-
-        def step(i, carry):
+        def product(p, total):
+            term = jnp.dot(tiles[slot_ref[p]], win[c][column_ref[p]], preferred_element_type=F32)
+            total = total * keep_ref[p] + term
+            part[p + 1] = total
+            return total
+
+        def step(i, total):
             for k in range(4):
-                product(i * 4 + k, carry)
-            return carry
-
-        lax.fori_loop(0, slots // 4, step, 0)
-        for t in range(slots // 4 * 4, slots):
-            product(t, 0)
-
-        def chain(t, carry):
-            part[t + 1] = part[t + 1] + part[prev_ref[t]]
-            return carry
-
-        lax.fori_loop(0, slots, chain, 0)
+                total = product(i * 4 + k, total)
+            return total
+
+        total = lax.fori_loop(0, slots // 4, step, jnp.zeros((tile, LANES), F32))
+        for p in range(slots // 4 * 4, slots):
+            total = product(p, total)
         for r in range(blocks):
             aggregated[c, r] = part[last_ref[r]].astype(BF16)
-        for d in range(1, snaps):
-            agg_to(c, d).start()
+        for p in peers:
+            agg_with(c, p).start()
         resident_agg[c, s] = aggregated[c, s]
 
     for copy in local:
@@ -230,14 +286,24 @@
 
     def pass_on(c):
         for d in range(2):
-            own(c, d).wait_recv()
-            relay(c, d).start()
+
+            @pl.when(receives[d])
+            def _():
+                own(c, d).wait_recv()
+
+            @pl.when(has_both)
+            def _():
+                relay(c, d).start()
+
             if c + 2 < chunks:
-                own(c + 2, d).start()
+                start_own(c + 2, d)
 
     def arrived(c):
         for d in range(2):
-            relay(c, d).wait_recv()
+
+            @pl.when(receives_far[d])
+            def _():
+                relay(c, d).wait_recv()
 
     pass_on(0)
     pass_on(1)
@@ -248,36 +314,36 @@
             pass_on(c + 2)
         if c == chunks - 2:
             for c2 in range(2):
-                for d in range(1, snaps):
-                    agg_to(c2, d).wait_recv()
+                for p in peers:
+                    agg_from(c2, p).wait_recv()
             for u in range(snaps):
-                pair = jnp.concatenate([resident_agg[0, u], resident_agg[1, u]], axis=1)
-                mixed[u] = jnp.dot(pair, wg[pl.ds(0, 2 * LANES)], preferred_element_type=F32)
-
-    for d in range(1, snaps):
-        feat_to(d).wait_recv()
-    for c2 in range(2, chunks):
-        for d in range(1, snaps):
-            agg_to(c2, d).wait_recv()
-
-    half = snaps // 2
-    rows = half * tile
-    for h in range(2):
-        for t in range(h * half, (h + 1) * half):
-            pair = jnp.concatenate([resident_agg[2, t], resident_agg[3, t]], axis=1)
-            total = mixed[t] + jnp.dot(pair, wg[pl.ds(2 * LANES, 2 * LANES)], preferred_element_type=F32)
-            hid = (resident_feat[t].astype(F32) + jnp.maximum(total, 0.0)).astype(BF16)
-            hidden[t] = hid
-            hid = hid.astype(F32)
-            mean = jnp.mean(hid, axis=-1, keepdims=True)
-            centred = hid - mean
-            variance = jnp.mean(centred * centred, axis=-1, keepdims=True)
-            normed[t] = (centred * lax.rsqrt(variance + 1e-05) * gain[...]).astype(BF16)
-        part_of = pl.ds(h * half, half)
-        some = normed[part_of].reshape(rows, width)
+                both = jnp.concatenate([resident_agg[0, u], resident_agg[1, u]], axis=1)
+                mixed[u] = jnp.dot(both, wg[pl.ds(0, 2 * LANES)], preferred_element_type=F32)
+            for p in peers:
+                feat_from(p).wait_recv()
+
+    rows = 2 * tile
+    for g in near_first:
+        for p in [other_core] if g == 0 else [pair_of[g], pair_of[g] + 1]:
+            for c in range(2, chunks):
+                agg_from(c, p).wait_recv()
+        pair = pl.ds(pair_of[g], 2)
+        both = jnp.concatenate(
+            [resident_agg[c, pair].reshape(rows, LANES) for c in range(2, chunks)], axis=1
+        )
+        total = jnp.dot(both, wg[pl.ds(2 * LANES, 2 * LANES)], preferred_element_type=F32)
+        total = mixed[pair].reshape(rows, width) + total
+        hid = resident_feat[pair].reshape(rows, width).astype(F32) + jnp.maximum(total, 0.0)
+        hid = hid.astype(BF16)
+        hidden[pair] = hid.reshape(2, tile, width)
+        hid = hid.astype(F32)
+        mean = jnp.mean(hid, axis=-1, keepdims=True)
+        centred = hid - mean
+        variance = jnp.mean(centred * centred, axis=-1, keepdims=True)
+        normed = (centred * lax.rsqrt(variance + 1e-05) * gain[...]).astype(BF16)
         for i, to in enumerate((query, key, value)):
-            product = jnp.dot(some, wqkv[i], preferred_element_type=F32).astype(BF16).astype(F32)
-            to[part_of] = product.reshape(half, tile, width)
+            product = jnp.dot(normed, wqkv[i], preferred_element_type=F32).astype(BF16).astype(F32)
+            to[pair] = product.reshape(2, tile, width)
 
     def column(u):
         return pl.ds(u * LANES, LANES)
@@ -327,6 +393,8 @@
 
     lax.fori_loop(0, tile // 16, context_rows, 0)
 
+    half = snaps // 2
+    rows = half * tile
     for h in range(2):
         part_of = pl.ds(h * half, half)
         projected = jnp.dot(context[part_of].reshape(rows, width), wo[...], preferred_element_type=F32)
@@ -336,12 +404,19 @@
 
     for c in range(chunks):
         for d in range(2):
-            own(c, d).wait_send()
-            relay(c, d).wait_send()
-        for d in range(1, snaps):
-            agg_to(c, d).wait_send()
-    for d in range(1, snaps):
-        feat_to(d).wait_send()
+
+            @pl.when(sends[d])
+            def _():
+                own(c, d).wait_send()
+
+            @pl.when(has_both)
+            def _():
+                relay(c, d).wait_send()
+
+        for p in peers:
+            agg_with(c, p).wait_send()
+    for p in peers:
+        feat_with(p).wait_send()
     for h in range(2):
         part_of = pl.ds(h * half, half)
         pltpu.make_async_copy(out_buf.at[part_of], out.at[part_of], out_sem.at[h]).wait()
@@ -396,21 +471,21 @@
             pltpu.VMEM((width, width), BF16),
             pltpu.VMEM((snaps * LANES, LANES), BF16),
             pltpu.VMEM((LANES, snaps * LANES), BF16),
-            pltpu.VMEM((snaps, tile, width), BF16),
             pltpu.VMEM((snaps, tile, snaps * LANES), BF16),
             pltpu.VMEM((snaps, tile, snaps * LANES), F32),
             pltpu.VMEM((snaps, tile, width), BF16),
             pltpu.VMEM((snaps, tile, width), BF16),
-            pltpu.SMEM((slots,), jnp.int32),
+            *[pltpu.SMEM((slots,), jnp.int32)] * 4,
+            pltpu.SMEM((slots,), F32),
             pltpu.SMEM((blocks,), jnp.int32),
             dma((2, chunks)),
             dma((2, chunks)),
             dma((2, chunks)),
             dma((2, chunks)),
-            dma((snaps - 1,)),
-            dma((snaps - 1,)),
-            dma((chunks, snaps - 1)),
-            dma((chunks, snaps - 1)),
+            dma((snaps,)),
+            dma((snaps,)),
+            dma((chunks, snaps)),
+            dma((chunks, snaps)),
             dma((8 + chunks,)),
             dma((snaps,)),
         ],

time: 82.5 us -> 78.6 us (0.953)
  the two profiles are of different devices: /device:TPU:1 before, /device:TPU:25 now
where the time goes in v3:
time: 78.6 us; the launch traced here: 78.4 us
  Pallas kernels  75.5 us (96%)
  local copies, waits for them, and re-layouts  2.26 us (3%)
    pallas_call x1, Pallas kernels, local_layer(): pl.pallas_call(kernel, out_shape=jax.ShapeDtypeStruct((snaps, tile, width...  75.5 us
    unnamed x1, local copies, waits for them, and re-layouts  2.26 us

profile of v3, /device:TPU:25, one launch (start us, length us, event | category | flops | bytes accessed | tf_op | source)
XLA Modules:
  0.0 78.4 jit_solution(8520749976190897213)
XLA Ops:
  0.7 75.5 %shard_map.109 = bf16[8,128,512]{2,1,0:T(8,128)(2,1)} custom-call(s32[1,28]{1,0:T(1,128)} %refs_0_.1, s32[1,28]{1,0:T(1,128)} %refs_1_.1, s32[1,1]{1,0:T(1,128)S(6)} %copy.13.refs_2_, bf16[8,128,512]{2,1,0:T(8,128)(2,1)} %bitcast.3, bf16[28,128,128]{2,1,0:T(8,128)(2,1)} %bitcast.4, bf16[512,512]{1,0:T(8,128)(2,1)} %refs_5_.1, f32[1,512]{1,0:T(1,128)} %bitcast.5, ...), custom_call_target="tpu_custom_call" | custom-call | flops 4000000000 | bytes 6291456 | tf_op jit(solution)/shard_map/pallas_call | solution.py:451
  76.1 2.3 %copy.14 = bf16[8,128,512]{2,1,0:T(8,128)(2,1)} copy(bf16[8,128,512]{2,1,0:T(8,128)(2,1)} %shard_map.109) | data formatting | bytes 2097152

commit v4 on v3

--- a/solution.py
+++ b/solution.py
@@ -46,12 +46,10 @@
     gain,
     wqkv,
     wo,
-    gather_heads,
-    spread_heads,
+    head_sum,
     partial,
-    wide,
+    scores,
     context,
-    out_buf,
     key_ref,
     rank_ref,
     slot_ref,
@@ -67,7 +65,6 @@
     agg_send,
     agg_recv,
     local_sem,
-    out_sem,
 ):
     win = (win_a, win_b, win_c, win_d)
     blocks = feat.shape[0]
@@ -75,7 +72,6 @@
     width = feat.shape[2]
     chunks = width // LANES
     group = LANES // HEADS
-    period = snaps * HEADS
     slots = tiles.shape[0]
     s = lax.axis_index("snap")
     j = lax.axis_index("node")
@@ -244,14 +240,10 @@
     order = jnp.where(source == moved, 1.0, 0.0).astype(BF16)
     moved = lax.rem(source, HEADS) * HEAD_DIM + source // LANES * group + lax.rem(source, LANES) // HEADS
     order_back = jnp.where(place == moved, 1.0, 0.0).astype(BF16)
-    lane = lax.broadcasted_iota(jnp.int32, (snaps * LANES, LANES), 1)
-    row = lax.broadcasted_iota(jnp.int32, (snaps * LANES, LANES), 0)
-    hit = lax.rem(lane, period) == row // LANES * HEADS + lax.rem(row, HEADS)
-    gather_heads[...] = jnp.where(hit, HEAD_DIM**-0.5, 0.0).astype(BF16)
-    lane = lax.broadcasted_iota(jnp.int32, (LANES, snaps * LANES), 1)
-    row = lax.broadcasted_iota(jnp.int32, (LANES, snaps * LANES), 0)
-    hit = row == lane // LANES * HEADS + lax.rem(lane, HEADS)
-    spread_heads[...] = jnp.where(hit, 1.0, 0.0).astype(BF16)
+    lane = lax.broadcasted_iota(jnp.int32, (2 * LANES, 2 * LANES), 1)
+    row = lax.broadcasted_iota(jnp.int32, (2 * LANES, 2 * LANES), 0)
+    hit = (lane // LANES == row // LANES) & (lax.rem(lane, HEADS) == lax.rem(row, HEADS))
+    head_sum[...] = jnp.where(hit, HEAD_DIM**-0.5, 0.0).astype(BF16)
     partial[...] = jnp.zeros(partial.shape, BF16)
     for copy in weights:
         copy.wait()
@@ -360,34 +352,31 @@
 
     lax.fori_loop(0, tile // 16, score_rows, 0)
 
-    lane = lax.broadcasted_iota(jnp.int32, (snaps, tile, LANES), 2)
-    of_row = lax.broadcasted_iota(jnp.int32, (snaps, tile, LANES), 0)
-    visible = (lax.rem(lane, period) // HEADS <= of_row).reshape(snaps * tile, LANES)
-    scores = jnp.dot(
-        partial[...].reshape(snaps * tile, snaps * LANES), gather_heads[...], preferred_element_type=F32
-    )
-    scores = jnp.where(visible, scores, -1e30)
-    top = scores
-    shift = HEADS
-    while shift < period:
-        top = jnp.maximum(top, pltpu.roll(top, shift, 1))
-        shift *= 2
-    e = jnp.exp(scores - top)
-    total = e
-    shift = HEADS
-    while shift < period:
-        total = total + pltpu.roll(total, shift, 1)
-        shift *= 2
-    w = (e / total).astype(BF16)
-    wide[...] = jnp.dot(w, spread_heads[...], preferred_element_type=F32).reshape(wide.shape)
+    for u in range(0, snaps, 2):
+        at = pl.ds(u * LANES, 2 * LANES)
+        later = (snaps - u) * tile
+        summed = jnp.dot(
+            partial[u:, :, at].reshape(later, 2 * LANES), head_sum[...], preferred_element_type=F32
+        )
+        scores[u:, :, at] = summed.reshape(snaps - u, tile, 2 * LANES)
 
     def context_rows(i, carry):
         at = pl.ds(pl.multiple_of(i * 16, 16), 16)
         for t in range(snaps):
+            row = [scores[t, at, column(u)] for u in range(t + 1)]
+            top = row[0]
+            for x in row[1:]:
+                top = jnp.maximum(top, x)
+            row = [jnp.exp(x - top) for x in row]
+            total = row[0]
+            for x in row[1:]:
+                total = total + x
+            scale = 1.0 / total
+            row = [(x * scale).astype(BF16).astype(F32) for x in row]
             for v in range(chunks):
-                total = wide[t, at, column(0)] * value[0, at, column(v)]
+                total = row[0] * value[0, at, column(v)]
                 for u in range(1, t + 1):
-                    total = total + wide[t, at, column(u)] * value[u, at, column(v)]
+                    total = total + row[u] * value[u, at, column(v)]
                 context[t, at, column(v)] = total.astype(BF16)
         return carry
 
@@ -399,8 +388,7 @@
         part_of = pl.ds(h * half, half)
         projected = jnp.dot(context[part_of].reshape(rows, width), wo[...], preferred_element_type=F32)
         result = hidden[part_of].astype(F32) + projected.reshape(half, tile, width)
-        out_buf[part_of] = result.astype(BF16)
-        pltpu.make_async_copy(out_buf.at[part_of], out.at[part_of], out_sem.at[h]).start()
+        out[part_of] = result.astype(BF16)
 
     for c in range(chunks):
         for d in range(2):
@@ -417,9 +405,6 @@
             agg_with(c, p).wait_send()
     for p in peers:
         feat_with(p).wait_send()
-    for h in range(2):
-        part_of = pl.ds(h * half, half)
-        pltpu.make_async_copy(out_buf.at[part_of], out.at[part_of], out_sem.at[h]).wait()
 
 
 def local_layer(
@@ -450,9 +435,9 @@
 
     return pl.pallas_call(
         kernel,
-        out_shape=jax.ShapeDtypeStruct((snaps, tile, width), BF16),
+        out_shape=pltpu.VMEM((snaps, tile, width), BF16),
         in_specs=[smem] * 3 + [hbm] * 8,
-        out_specs=hbm,
+        out_specs=pl.BlockSpec(memory_space=pltpu.VMEM),
         scratch_shapes=[
             *[pltpu.VMEM((5 * blocks, tile, LANES), BF16)] * chunks,
             pltpu.VMEM((slots, tile, tile), BF16),
@@ -469,11 +454,9 @@
             pltpu.VMEM((1, width), F32),
             pltpu.VMEM((3, width, width), BF16),
             pltpu.VMEM((width, width), BF16),
-            pltpu.VMEM((snaps * LANES, LANES), BF16),
-            pltpu.VMEM((LANES, snaps * LANES), BF16),
+            pltpu.VMEM((2 * LANES, 2 * LANES), BF16),
             pltpu.VMEM((snaps, tile, snaps * LANES), BF16),
             pltpu.VMEM((snaps, tile, snaps * LANES), F32),
-            pltpu.VMEM((snaps, tile, width), BF16),
             pltpu.VMEM((snaps, tile, width), BF16),
             *[pltpu.SMEM((slots,), jnp.int32)] * 4,
             pltpu.SMEM((slots,), F32),
@@ -487,10 +470,9 @@
             dma((chunks, snaps)),
             dma((chunks, snaps)),
             dma((8 + chunks,)),
-            dma((snaps,)),
         ],
         compiler_params=pltpu.CompilerParams(
-            collective_id=0, has_side_effects=True, vmem_limit_bytes=60 * 2**20
+            collective_id=0, has_side_effects=True, vmem_limit_bytes=58 * 2**20
         ),
         cost_estimate=pl.CostEstimate(
             flops=4 * 10**9, bytes_accessed=6 * 2**20, transcendentals=10**6

time: 78.6 us -> 74.7 us (0.950)
  Pallas kernels: 75.5 us -> 73 us
  local copies, waits for them, and re-layouts: 2.26 us -> 0.97 us
    pallas_call x1, Pallas kernels: 75.5 us -> 73 us  [local_layer(): pl.pallas_call(kernel, out_shape=pltpu.VMEM((snaps, tile, width), BF16),...]
    unnamed x1, local copies, waits for them, and re-layouts: 2.26 us -> 0.97 us
where the time goes in v4:
time: 74.7 us; the launch traced here: 74.6 us
  Pallas kernels  73 us (98%)
  local copies, waits for them, and re-layouts  0.97 us (1%)
    pallas_call x1, Pallas kernels, local_layer(): pl.pallas_call(kernel, out_shape=pltpu.VMEM((snaps, tile, width), BF16),...  73 us

profile of v4, /device:TPU:25, one launch (start us, length us, event | category | flops | bytes accessed | tf_op | source)
XLA Modules:
  0.0 74.6 jit_solution(3905784374621597283)
XLA Ops:
  0.7 73.0 %shard_map.109 = bf16[8,128,512]{2,1,0:T(8,128)(2,1)S(1)} custom-call(s32[1,28]{1,0:T(1,128)} %refs_0_.1, s32[1,28]{1,0:T(1,128)} %refs_1_.1, s32[1,1]{1,0:T(1,128)S(6)} %copy.14.refs_2_, bf16[8,128,512]{2,1,0:T(8,128)(2,1)} %bitcast.3, bf16[28,128,128]{2,1,0:T(8,128)(2,1)} %bitcast.4, bf16[512,512]{1,0:T(8,128)(2,1)} %refs_5_.1, f32[1,512]{1,0:T(1,128)} %bitcast.5, ...), custom_call_target="tpu_custom_call" | custom-call | flops 4000000000 | bytes 6291456 | tf_op jit(solution)/shard_map/pallas_call | solution.py:436
  73.6 1.0 %copy.13 = bf16[8,128,512]{2,1,0:T(8,128)(2,1)} copy(bf16[8,128,512]{2,1,0:T(8,128)(2,1)S(1)} %shard_map.109) | data formatting | bytes 2097152

commit v5 on v4

--- a/solution.py
+++ b/solution.py
@@ -32,10 +32,14 @@
     win_b,
     win_c,
     win_d,
+    win_e,
+    last_columns,
     tiles,
     part,
     aggregated,
     resident_agg,
+    aggregated_narrow,
+    resident_narrow,
     resident_feat,
     mixed,
     hidden,
@@ -66,11 +70,13 @@
     agg_recv,
     local_sem,
 ):
-    win = (win_a, win_b, win_c, win_d)
+    win = (win_a, win_b, win_c, win_d, win_e)
     blocks = feat.shape[0]
     tile = feat.shape[1]
     width = feat.shape[2]
     chunks = width // LANES
+    narrow = LANES // 2
+    sent = chunks + 1
     group = LANES // HEADS
     slots = tiles.shape[0]
     s = lax.axis_index("snap")
@@ -90,11 +96,8 @@
 
     local = [pltpu.make_async_copy(tiles_hbm, tiles, local_sem.at[0])]
     for c in range(chunks):
-        local.append(
-            pltpu.make_async_copy(
-                feat.at[:, :, cols_of(c)], win[c].at[pl.ds(2 * blocks, blocks)], local_sem.at[1 + c]
-            )
-        )
+        place = last_columns if c == chunks - 1 else win[c].at[pl.ds(2 * blocks, blocks)]
+        local.append(pltpu.make_async_copy(feat.at[:, :, cols_of(c)], place, local_sem.at[1 + c]))
     base = 1 + chunks
     weights = [
         pltpu.make_async_copy(wg_hbm, wg, local_sem.at[base]),
@@ -108,7 +111,7 @@
 
     def own(c, d):
         return pltpu.make_async_remote_copy(
-            src_ref=feat.at[:, :, cols_of(c)],
+            src_ref=feat.at[:, :, cols_of(c)] if c < chunks - 1 else win[c].at[pl.ds(2 * blocks, blocks)],
             dst_ref=win[c].at[pl.ds(near[d], blocks)],
             send_sem=own_send.at[d, c],
             recv_sem=own_recv.at[d, c],
@@ -146,10 +149,16 @@
             device_id_type=MESH,
         )
 
+    def agg_at(c, p):
+        return aggregated.at[c, p] if c < chunks - 1 else aggregated_narrow.at[c - chunks + 1, p]
+
+    def resident_at(c, p):
+        return resident_agg.at[c, p] if c < chunks - 1 else resident_narrow.at[c - chunks + 1, p]
+
     def agg_with(c, p):
         return pltpu.make_async_remote_copy(
-            src_ref=aggregated.at[c, p],
-            dst_ref=resident_agg.at[c, s],
+            src_ref=agg_at(c, p),
+            dst_ref=resident_at(c, s),
             send_sem=agg_send.at[c, p],
             recv_sem=agg_recv.at[c, s],
             device_id=(p, j),
@@ -158,8 +167,8 @@
 
     def agg_from(c, p):
         return pltpu.make_async_remote_copy(
-            src_ref=aggregated.at[c, p],
-            dst_ref=resident_agg.at[c, p],
+            src_ref=agg_at(c, p),
+            dst_ref=resident_at(c, p),
             send_sem=agg_send.at[c, p],
             recv_sem=agg_recv.at[c, p],
             device_id=(p, j),
@@ -200,6 +209,22 @@
             start_own(c, d)
     for p in peers:
         feat_with(p).start()
+
+    for copy in local:
+        copy.wait()
+
+    def lanes_swapped(x):
+        return pltpu.roll(x.astype(F32), narrow, x.ndim - 1)
+
+    def in_left_lanes(shape):
+        return lax.broadcasted_iota(jnp.int32, shape, len(shape) - 1) < narrow
+
+    for b in range(blocks):
+        upper = last_columns[b, :narrow].astype(F32)
+        lower = last_columns[b, narrow:].astype(F32)
+        left = in_left_lanes(upper.shape)
+        win_d[2 * blocks + b] = jnp.where(left, upper, lanes_swapped(lower)).astype(BF16)
+        win_e[2 * blocks + b] = jnp.where(left, lanes_swapped(upper), lower).astype(BF16)
 
     live_slots = count_ref[0, 0]
 
@@ -252,29 +277,40 @@
     wo[...] = jnp.dot(order_back, wo[...], preferred_element_type=F32).astype(BF16)
     part[0] = jnp.zeros((tile, LANES), F32)
 
+    unroll = 14
+
     def aggregate(c):
         def product(p, total):
-            term = jnp.dot(tiles[slot_ref[p]], win[c][column_ref[p]], preferred_element_type=F32)
+            source = win[c][column_ref[p]]
+            if c >= chunks - 1:
+                source = jnp.concatenate([source, lanes_swapped(source).astype(BF16)], axis=0)
+            term = jnp.dot(tiles[slot_ref[p]], source, preferred_element_type=F32)
             total = total * keep_ref[p] + term
             part[p + 1] = total
             return total
 
         def step(i, total):
-            for k in range(4):
-                total = product(i * 4 + k, total)
+            for k in range(unroll):
+                total = product(i * unroll + k, total)
             return total
 
-        total = lax.fori_loop(0, slots // 4, step, jnp.zeros((tile, LANES), F32))
-        for p in range(slots // 4 * 4, slots):
+        total = lax.fori_loop(0, slots // unroll, step, jnp.zeros((tile, LANES), F32))
+        for p in range(slots // unroll * unroll, slots):
             total = product(p, total)
         for r in range(blocks):
-            aggregated[c, r] = part[last_ref[r]].astype(BF16)
+            total = part[last_ref[r]]
+            if c < chunks - 1:
+                aggregated[c, r] = total.astype(BF16)
+            else:
+                upper, lower = total[:narrow], lanes_swapped(total[narrow:])
+                packed = jnp.where(in_left_lanes(upper.shape), upper, lower)
+                aggregated_narrow[c - chunks + 1, r] = packed.astype(BF16)
         for p in peers:
             agg_with(c, p).start()
-        resident_agg[c, s] = aggregated[c, s]
-
-    for copy in local:
-        copy.wait()
+        if c < chunks - 1:
+            resident_agg[c, s] = aggregated[c, s]
+        else:
+            resident_narrow[c - chunks + 1, s] = aggregated_narrow[c - chunks + 1, s]
 
     def pass_on(c):
         for d in range(2):
@@ -287,7 +323,7 @@
             def _():
                 relay(c, d).start()
 
-            if c + 2 < chunks:
+            if c + 2 < sent:
                 start_own(c + 2, d)
 
     def arrived(c):
@@ -297,14 +333,32 @@
             def _():
                 relay(c, d).wait_recv()
 
+    def own_sent(c):
+        for d in range(2):
+
+            @pl.when(sends[d])
+            def _():
+                own(c, d).wait_send()
+
+    def relay_sent(c):
+        for d in range(2):
+
+            @pl.when(has_both)
+            def _():
+                relay(c, d).wait_send()
+
+    def agg_sent(c):
+        for p in peers:
+            agg_with(c, p).wait_send()
+
     pass_on(0)
     pass_on(1)
-    for c in range(chunks):
+    for c in range(sent):
         arrived(c)
         aggregate(c)
-        if c + 2 < chunks:
+        if c + 2 < sent:
             pass_on(c + 2)
-        if c == chunks - 2:
+        if c == 2:
             for c2 in range(2):
                 for p in peers:
                     agg_from(c2, p).wait_recv()
@@ -313,15 +367,30 @@
                 mixed[u] = jnp.dot(both, wg[pl.ds(0, 2 * LANES)], preferred_element_type=F32)
             for p in peers:
                 feat_from(p).wait_recv()
-
+            for p in peers:
+                feat_with(p).wait_send()
+            for c2 in range(2):
+                relay_sent(c2)
+                agg_sent(c2)
+            for c2 in range(sent - 1):
+                own_sent(c2)
+
+    own_sent(sent - 1)
+    relay_sent(2)
+    agg_sent(2)
     rows = 2 * tile
     for g in near_first:
         for p in [other_core] if g == 0 else [pair_of[g], pair_of[g] + 1]:
-            for c in range(2, chunks):
+            for c in range(2, sent):
                 agg_from(c, p).wait_recv()
         pair = pl.ds(pair_of[g], 2)
+        first, second = resident_narrow[0, pair].astype(F32), resident_narrow[1, pair].astype(F32)
+        left = in_left_lanes(first.shape)
+        upper = jnp.where(left, first, lanes_swapped(second))
+        lower = jnp.where(left, lanes_swapped(first), second)
+        joined = jnp.concatenate([upper, lower], axis=1).astype(BF16)
         both = jnp.concatenate(
-            [resident_agg[c, pair].reshape(rows, LANES) for c in range(2, chunks)], axis=1
+            [resident_agg[2, pair].reshape(rows, LANES), joined.reshape(rows, LANES)], axis=1
         )
         total = jnp.dot(both, wg[pl.ds(2 * LANES, 2 * LANES)], preferred_element_type=F32)
         total = mixed[pair].reshape(rows, width) + total
@@ -390,21 +459,9 @@
         result = hidden[part_of].astype(F32) + projected.reshape(half, tile, width)
         out[part_of] = result.astype(BF16)
 
-    for c in range(chunks):
-        for d in range(2):
-
-            @pl.when(sends[d])
-            def _():
-                own(c, d).wait_send()
-
-            @pl.when(has_both)
-            def _():
-                relay(c, d).wait_send()
-
-        for p in peers:
-            agg_with(c, p).wait_send()
-    for p in peers:
-        feat_with(p).wait_send()
+    for c in range(3, sent):
+        relay_sent(c)
+        agg_sent(c)
 
 
 def local_layer(
@@ -439,11 +496,15 @@
         in_specs=[smem] * 3 + [hbm] * 8,
         out_specs=pl.BlockSpec(memory_space=pltpu.VMEM),
         scratch_shapes=[
-            *[pltpu.VMEM((5 * blocks, tile, LANES), BF16)] * chunks,
+            *[pltpu.VMEM((5 * blocks, tile, LANES), BF16)] * (chunks - 1),
+            *[pltpu.VMEM((5 * blocks, tile // 2, LANES), BF16)] * 2,
+            pltpu.VMEM((blocks, tile, LANES), BF16),
             pltpu.VMEM((slots, tile, tile), BF16),
             pltpu.VMEM((slots + 1, tile, LANES), F32),
-            pltpu.VMEM((chunks, blocks, tile, LANES), BF16),
-            pltpu.VMEM((chunks, snaps, tile, LANES), BF16),
+            pltpu.VMEM((chunks - 1, blocks, tile, LANES), BF16),
+            pltpu.VMEM((chunks - 1, snaps, tile, LANES), BF16),
+            pltpu.VMEM((2, blocks, tile // 2, LANES), BF16),
+            pltpu.VMEM((2, snaps, tile // 2, LANES), BF16),
             pltpu.VMEM((snaps, tile, width), BF16),
             pltpu.VMEM((snaps, tile, width), F32),
             pltpu.VMEM((snaps, tile, width), BF16),
@@ -461,14 +522,14 @@
             *[pltpu.SMEM((slots,), jnp.int32)] * 4,
             pltpu.SMEM((slots,), F32),
             pltpu.SMEM((blocks,), jnp.int32),
-            dma((2, chunks)),
-            dma((2, chunks)),
-            dma((2, chunks)),
-            dma((2, chunks)),
+            dma((2, chunks + 1)),
+            dma((2, chunks + 1)),
+            dma((2, chunks + 1)),
+            dma((2, chunks + 1)),
             dma((snaps,)),
             dma((snaps,)),
-            dma((chunks, snaps)),
-            dma((chunks, snaps)),
+            dma((chunks + 1, snaps)),
+            dma((chunks + 1, snaps)),
             dma((8 + chunks,)),
         ],
         compiler_params=pltpu.CompilerParams(

time: 74.7 us -> 73.5 us (0.984)
  Pallas kernels: 73 us -> 71.8 us
    pallas_call x1, Pallas kernels: 73 us -> 71.8 us  [local_layer(): pl.pallas_call(kernel, out_shape=pltpu.VMEM((snaps, tile, width), BF16),...]
where the time goes in v5:
time: 73.5 us; the launch traced here: 73.4 us
  Pallas kernels  71.8 us (98%)
  local copies, waits for them, and re-layouts  0.97 us (1%)
    pallas_call x1, Pallas kernels, local_layer(): pl.pallas_call(kernel, out_shape=pltpu.VMEM((snaps, tile, width), BF16),...  71.8 us

profile of v5, /device:TPU:25, one launch (start us, length us, event | category | flops | bytes accessed | tf_op | source)
XLA Modules:
  0.0 73.4 jit_solution(2612980314164192076)
XLA Ops:
  0.7 71.8 %shard_map.109 = bf16[8,128,512]{2,1,0:T(8,128)(2,1)S(1)} custom-call(s32[1,28]{1,0:T(1,128)} %refs_0_.1, s32[1,28]{1,0:T(1,128)} %refs_1_.1, s32[1,1]{1,0:T(1,128)S(6)} %copy.14.refs_2_, bf16[8,128,512]{2,1,0:T(8,128)(2,1)} %bitcast.3, bf16[28,128,128]{2,1,0:T(8,128)(2,1)} %bitcast.4, bf16[512,512]{1,0:T(8,128)(2,1)} %refs_5_.1, f32[1,512]{1,0:T(1,128)} %bitcast.5, ...), custom_call_target="tpu_custom_call" | custom-call | flops 4000000000 | bytes 6291456 | tf_op jit(solution)/shard_map/pallas_call | solution.py:493
  72.4 1.0 %copy.13 = bf16[8,128,512]{2,1,0:T(8,128)(2,1)} copy(bf16[8,128,512]{2,1,0:T(8,128)(2,1)S(1)} %shard_map.109) | data formatting | bytes 2097152

commit v6 on v5

--- a/solution.py
+++ b/solution.py
@@ -403,7 +403,7 @@
         variance = jnp.mean(centred * centred, axis=-1, keepdims=True)
         normed = (centred * lax.rsqrt(variance + 1e-05) * gain[...]).astype(BF16)
         for i, to in enumerate((query, key, value)):
-            product = jnp.dot(normed, wqkv[i], preferred_element_type=F32).astype(BF16).astype(F32)
+            product = jnp.dot(normed, wqkv[i], preferred_element_type=F32)
             to[pair] = product.reshape(2, tile, width)
 
     def column(u):
@@ -419,7 +419,7 @@
                 partial[t, at, column(u)] = total.astype(BF16)
         return carry
 
-    lax.fori_loop(0, tile // 16, score_rows, 0)
+    lax.fori_loop(0, tile // 32, lambda i, x: score_rows(2 * i + 1, score_rows(2 * i, x)), 0)
 
     for u in range(0, snaps, 2):
         at = pl.ds(u * LANES, 2 * LANES)
@@ -441,7 +441,7 @@
             for x in row[1:]:
                 total = total + x
             scale = 1.0 / total
-            row = [(x * scale).astype(BF16).astype(F32) for x in row]
+            row = [x * scale for x in row]
             for v in range(chunks):
                 total = row[0] * value[0, at, column(v)]
                 for u in range(1, t + 1):
@@ -449,7 +449,7 @@
                 context[t, at, column(v)] = total.astype(BF16)
         return carry
 
-    lax.fori_loop(0, tile // 16, context_rows, 0)
+    lax.fori_loop(0, tile // 32, lambda i, x: context_rows(2 * i + 1, context_rows(2 * i, x)), 0)
 
     half = snaps // 2
     rows = half * tile

time: 73.5 us -> 73.3 us (level)
  no operation moved by 1% of the time
where the time goes in v6:
time: 73.3 us; the launch traced here: 73.2 us
  Pallas kernels  71.5 us (98%)
  local copies, waits for them, and re-layouts  0.97 us (1%)
    pallas_call x1, Pallas kernels, local_layer(): pl.pallas_call(kernel, out_shape=pltpu.VMEM((snaps, tile, width), BF16),...  71.5 us

profile of v6, /device:TPU:25, one launch (start us, length us, event | category | flops | bytes accessed | tf_op | source)
XLA Modules:
  0.0 73.2 jit_solution(1681972014003309244)
XLA Ops:
  0.7 71.5 %shard_map.109 = bf16[8,128,512]{2,1,0:T(8,128)(2,1)S(1)} custom-call(s32[1,28]{1,0:T(1,128)} %refs_0_.1, s32[1,28]{1,0:T(1,128)} %refs_1_.1, s32[1,1]{1,0:T(1,128)S(6)} %copy.14.refs_2_, bf16[8,128,512]{2,1,0:T(8,128)(2,1)} %bitcast.3, bf16[28,128,128]{2,1,0:T(8,128)(2,1)} %bitcast.4, bf16[512,512]{1,0:T(8,128)(2,1)} %refs_5_.1, f32[1,512]{1,0:T(1,128)} %bitcast.5, ...), custom_call_target="tpu_custom_call" | custom-call | flops 4000000000 | bytes 6291456 | tf_op jit(solution)/shard_map/pallas_call | solution.py:493
  72.2 1.0 %copy.13 = bf16[8,128,512]{2,1,0:T(8,128)(2,1)} copy(bf16[8,128,512]{2,1,0:T(8,128)(2,1)S(1)} %shard_map.109) | data formatting | bytes 2097152

commit v7 on v6

--- a/solution.py
+++ b/solution.py
@@ -277,7 +277,7 @@
     wo[...] = jnp.dot(order_back, wo[...], preferred_element_type=F32).astype(BF16)
     part[0] = jnp.zeros((tile, LANES), F32)
 
-    unroll = 14
+    unroll = 28
 
     def aggregate(c):
         def product(p, total):

time: 73.3 us -> 73.1 us (level)
  no operation moved by 1% of the time
where the time goes in v7:
time: 73.1 us; the launch traced here: 72.9 us
  Pallas kernels  71.3 us (98%)
  local copies, waits for them, and re-layouts  0.97 us (1%)
    pallas_call x1, Pallas kernels, local_layer(): pl.pallas_call(kernel, out_shape=pltpu.VMEM((snaps, tile, width), BF16),...  71.3 us

profile of v7, /device:TPU:25, one launch (start us, length us, event | category | flops | bytes accessed | tf_op | source)
XLA Modules:
  0.0 72.9 jit_solution(16957700615910892484)
XLA Ops:
  0.7 71.3 %shard_map.109 = bf16[8,128,512]{2,1,0:T(8,128)(2,1)S(1)} custom-call(s32[1,28]{1,0:T(1,128)} %refs_0_.1, s32[1,28]{1,0:T(1,128)} %refs_1_.1, s32[1,1]{1,0:T(1,128)S(6)} %copy.14.refs_2_, bf16[8,128,512]{2,1,0:T(8,128)(2,1)} %bitcast.3, bf16[28,128,128]{2,1,0:T(8,128)(2,1)} %bitcast.4, bf16[512,512]{1,0:T(8,128)(2,1)} %refs_5_.1, f32[1,512]{1,0:T(1,128)} %bitcast.5, ...), custom_call_target="tpu_custom_call" | custom-call | flops 4000000000 | bytes 6291456 | tf_op jit(solution)/shard_map/pallas_call | solution.py:493
  72.0 1.0 %copy.13 = bf16[8,128,512]{2,1,0:T(8,128)(2,1)} copy(bf16[8,128,512]{2,1,0:T(8,128)(2,1)S(1)} %shard_map.109) | data formatting | bytes 2097152
